TPU v7x, 128 devices: a whole 4x4x4 slice. The times are simulated.
128 devices in a mesh: tm: 8 (over x_lo, y), gx: 4 (over x_hi, core), gy: 4 (over z).
Axes of the slice: x: 4 (x_hi: 2, x_lo: 2; x = x_hi * 2 + x_lo), y: 4, z: 4, core: 2. Of those that a mesh axis runs over, the one named last changes fastest.
Arguments:
- guess: float32 [3, 8, 64, 64, 256], P(None, 'tm', 'gx', 'gy'), may hold values from -1 to 1
Outputs:
- updated: float32 [3, 8, 64, 64, 256], P(None, 'tm', 'gx', 'gy')
All inputs are finite; a program needn't handle non-finite values.
Results may differ from a plain program's by a relative error of at most 0.0001.
Values sent between devices are 32-bit elements; how exact they have to be, the bound alone decides.
A program may use at most 128 MiB of HBM per device.

v0:
```python
import jax
import jax.numpy as jnp
from jax import lax
from jax.sharding import PartitionSpec as P

KAPPA = 1.0
STEP = 0.01
HALF_STEP = 0.005
WEIGHTS = ((5.0 / 24.0, 1.0 / 3.0, -1.0 / 24.0), (-1.0 / 24.0, 1.0 / 3.0, 5.0 / 24.0))


def with_halo(block, sides, width):
    for axis, dim in sides:
        count = lax.axis_size(axis)
        forward = [(i, i + 1) for i in range(count - 1)]
        forward.append((count - 1, 0))
        backward = [(target, source) for source, target in forward]
        low = lax.ppermute(
            lax.slice_in_dim(block, block.shape[dim] - width, None, axis=dim), axis, forward
        )
        high = lax.ppermute(lax.slice_in_dim(block, 0, width, axis=dim), axis, backward)
        block = jnp.concatenate([low, block, high], axis=dim)
    return block


def passed_along(value, axis, by):
    length = lax.axis_size(axis)
    pairs = [(i, i + by) for i in range(length) if 0 <= i + by < length]
    return lax.ppermute(value, axis, pairs)


def laplace_padded(padded, inverse):
    center = padded[:, 1:-1, 1:-1]
    beside = padded[:, 2:, 1:-1] + padded[:, :-2, 1:-1]
    beside = beside + padded[:, 1:-1, 2:] + padded[:, 1:-1, :-2]
    beside = beside + jnp.roll(center, -1, 3) + jnp.roll(center, 1, 3)
    return (beside - 6.0 * center) * inverse


def tendency(values, inverse):
    padded = with_halo(values, (("gx", 1), ("gy", 2)), 1)
    potential = values * values * values - values - KAPPA * laplace_padded(padded, inverse)
    widened = with_halo(potential, (("gx", 1), ("gy", 2)), 1)
    return laplace_padded(widened, inverse)


def integrals(forces):
    return [
        STEP
        * (
            WEIGHTS[node][0] * forces[0]
            + WEIGHTS[node][1] * forces[1]
            + WEIGHTS[node][2] * forces[2]
        )
        for node in range(2)
    ]


def sdc_sweep(start, old_forces, parts, inverse, start_force):
    nodes = [start]
    forces = []
    current = start
    for node in range(2):
        if node == 0 and start_force is not None:
            now = start_force
        else:
            now = tendency(current, inverse)
        forces.append(now)
        current = current + HALF_STEP * (now - old_forces[node]) + parts[node]
        nodes.append(current)
    return (nodes, forces)


def restrict(field):
    count, sx, sy, sz = field.shape
    return jnp.mean(field.reshape(count, sx // 2, 2, sy // 2, 2, sz // 2, 2), axis=(2, 4, 6))


def prolong(field):
    count, sx, sy, sz = field.shape
    wide = jnp.broadcast_to(field[:, :, None, :, None, :, None], (count, sx, 2, sy, 2, sz, 2))
    return wide.reshape(count, sx * 2, sy * 2, sz * 2)


def local(guess):
    nodes = guess[:, 0]
    first_slice = lax.axis_index("tm") == 0
    received = passed_along(nodes[2:3], "tm", 1)
    start = jnp.where(first_slice, nodes[0:1], received)
    initial_forces = tendency(nodes, 1.0)
    old = [initial_forces[j : j + 1] for j in range(3)]
    first_nodes, first_forces = sdc_sweep(start, old, integrals(old), 1.0, None)
    old = first_forces + [tendency(first_nodes[2], 1.0)]
    second_nodes, second_forces = sdc_sweep(start, old, integrals(old), 1.0, first_forces[0])
    fine_forces = second_forces + [tendency(second_nodes[2], 1.0)]
    fine_stack = jnp.concatenate(second_nodes, axis=0)
    coarse_nodes = restrict(fine_stack)
    coarse_forces = restrict(jnp.concatenate(fine_forces, axis=0))
    coarse_parts = integrals([coarse_forces[j : j + 1] for j in range(3)])
    coarse_pair = tendency(coarse_nodes[0:2], 0.25)
    coarse_old = [coarse_pair[0:1], coarse_pair[1:2]]

    def coarse_sweep(initial):
        values, unused = sdc_sweep(initial, coarse_old, coarse_parts, 0.25, None)
        return tuple(values)

    def chain_turn(turn, carried):
        arrived = passed_along(carried[2], "tm", 1)
        initial = jnp.where(first_slice, coarse_nodes[0:1], arrived)
        return coarse_sweep(initial)

    values = coarse_sweep(coarse_nodes[0:1])
    values = lax.fori_loop(0, lax.axis_size("tm") - 1, chain_turn, values)
    coarse_final = jnp.concatenate(values, axis=0)
    updated = fine_stack + prolong(coarse_final - coarse_nodes)
    return updated[:, None]


def solution(mesh):
    placed = (P(None, "tm", "gx", "gy", None),)
    return jax.shard_map(
        local,
        mesh=mesh,
        in_specs=placed,
        out_specs=P(None, "tm", "gx", "gy", None),
        check_vma=False,
    )
```

profile of v0, /device:TPU:2, one launch (start us, length us, event | category | flops | bytes accessed | tf_op | source)
XLA Modules:
  0.0 728.2 jit_solution(1518215935935935531)
XLA Ops:
  1.0 3.5 collective-permute-start.17
  12.9 4.1 collective-permute-start.28
  18.8 3.6 collective-permute-done.29
  27.2 3.3 collective-permute-done.31
  39.2 3.3 collective-permute-done.19
  49.4 3.3 collective-permute-done.23
  59.7 3.3 collective-permute-done.35
  70.6 3.5 collective-permute-done.39
  81.1 3.3 collective-permute-done.43
  91.3 3.3 collective-permute-done.47
  101.6 3.3 collective-permute-done.51
  112.5 3.3 collective-permute-done.55
  121.6 51.6 %reshape.85 = f32[3,8,2,8,2,128,2]{6,5,4,3,2,1,0:T(8,128)} reshape(f32[3,16,16,256]{3,2,1,0:T(8,128)S(1)} %pad_maximum_fusion.60) | data formatting | bytes 1572864 | tf_op jit(solution)/shard_map/reshape | solution.py:76
  173.2 17.8 %reduce_sum.18 = f32[3,8,8,128]{3,2,1,0:T(8,128)S(1)} reduce(f32[3,8,2,8,2,128,2]{6,5,4,3,2,1,0:T(8,128)} %reshape.85, f32[]{:T(128)} %constant.9.clone.1), dimensions={2,4,6}, to_apply=%region_0.1 | reduce | flops 172032 | bytes 884740 | tf_op jit(solution)/shard_map/reduce_sum | solution.py:76
  233.3 3.3 collective-permute-done.81
  236.8 51.6 %reshape.86 = f32[3,8,2,8,2,128,2]{6,5,4,3,2,1,0:T(8,128)} reshape(f32[3,16,16,256]{3,2,1,0:T(8,128)S(1)} %pad_maximum_fusion.61) | data formatting | bytes 1572864 | tf_op jit(solution)/shard_map/reshape | solution.py:76
  288.4 17.8 %reduce_sum.19 = f32[3,8,8,128]{3,2,1,0:T(8,128)S(1)} reduce(f32[3,8,2,8,2,128,2]{6,5,4,3,2,1,0:T(8,128)} %reshape.86, f32[]{:T(128)} %constant.9.clone.1), dimensions={2,4,6}, to_apply=%region_1.2 | reduce | flops 172032 | bytes 884740 | tf_op jit(solution)/shard_map/reduce_sum | solution.py:76
  317.8 3.3 collective-permute-done.87
  326.2 347.6 %while.14 = (s32[]{:T(128)}, f32[1,8,8,128]{3,2,1,0:T(8,128)}, f32[1,8,8,128]{3,2,1,0:T(8,128)}, f32[1,8,8,128]{3,2,1,0:T(8,128)S(1)}, pred[]{:T(512)}, /*index=...) while((s32[]{:T(128)}, f32[1,8,8,128]{3,2,1,0:T(8,128)}, ...), condition=%wide.region_3.4_spmd, body=%wide.region_2.3_spmd.sunk | while | flops 749570 | bytes 2376526 | solution.py:113
  326.2 3.5 collective-permute-start
  329.7 5.6 collective-permute-done
  336.8 3.3 collective-permute-done.2
  378.8 6.0 collective-permute-done
  386.3 3.3 collective-permute-done.2
  428.3 6.0 collective-permute-done
  435.8 3.3 collective-permute-done.2
  477.8 6.0 collective-permute-done
  527.3 6.0 collective-permute-done
  576.8 6.0 collective-permute-done
  626.3 6.0 collective-permute-done
  674.6 16.5 %broadcast_in_dim.2 = f32[3,8,2,8,2,128,2]{6,5,4,3,2,1,0:T(8,128)} broadcast(f32[3,8,8,128]{3,2,1,0:T(8,128)S(1)} %maximum_subtract_fusion), dimensions={0,1,3,5} | broadcast | bytes 884736 | tf_op jit(solution)/shard_map/broadcast_in_dim | solution.py:81
  691.1 35.6 %reshape.87 = f32[3,1,16,16,256]{4,3,2,0,1:T(8,128)S(1)} reshape(f32[3,8,2,8,2,128,2]{6,5,4,3,2,1,0:T(8,128)} %broadcast_in_dim.2) | data formatting | bytes 1572864 | tf_op jit(solution)/shard_map/reshape | solution.py:82
  (639 shorter events, 432.6 us)
Async XLA Ops:
  1.0 35.7 %collective-permute-start.17 = (f32[1,16,16,256]{3,2,1,0:T(8,128)S(1)}, f32[1,16,16,256]{3,2,1,0:T(8,128)S(1)}, u32[]{:S(2)}, u32[]{:S(2)}) collective-permute-start(f32[1,16,16,256]{3,2,1,0:T(8,128)S(1)} %slice_bitcast_fusion), channel_id=1, source_target_pairs={{0,16},{16,32},{32,48},{48,64},{64,80},{80,96},{96,112},{1,17},{17... | collective-permute-start | bytes 786440 | tf_op jit(solution)/shard_map/ppermute | solution.py:29
  6.6 5.0 collective-permute-start.27
  12.9 5.9 collective-permute-start.28
  17.0 5.4 collective-permute-start.29
  25.4 5.1 collective-permute-start.31
  30.7 5.4 collective-permute-start.33
  42.6 5.0 collective-permute-start.21
  52.8 5.0 collective-permute-start.25
  63.9 5.0 collective-permute-start.37
  74.3 5.0 collective-permute-start.41
  94.8 5.0 collective-permute-start.49
  105.8 5.0 collective-permute-start.53
  116.0 5.0 collective-permute-start.57
  191.3 6.9 collective-permute-start.58
  191.3 6.9 collective-permute-start.59
  191.9 19.5 %collective-permute-start.74 = (f32[1,1,16,256]{3,2,1,0:T(8,128)S(1)}, f32[1,1,16,256]{3,2,1,0:T(8,128)S(1)}, u32[]{:S(2)}, u32[]{:S(2)}) collective-permute-start(f32[1,1,16,256]{3,2,1,0:T(8,128)S(1)} %get-tuple-element.171), channel_id=1, source_target_pairs={{4,0},{8,4},{12,8},{0,12},{5,1},{9,5},{13,9},{1,13},{6,2},{10,6},{... | collective-permute-start | bytes 49160 | tf_op jit(solution)/shard_map/ppermute | solution.py:21
  195.0 18.4 %collective-permute-start.75 = (f32[1,1,16,256]{3,2,1,0:T(8,128)S(1)}, f32[1,1,16,256]{3,2,1,0:T(8,128)S(1)}, u32[]{:S(2)}, u32[]{:S(2)}) collective-permute-start(f32[1,1,16,256]{3,2,1,0:T(8,128)S(1)} %get-tuple-element.170), channel_id=1, source_target_pairs={{0,4},{4,8},{8,12},{12,0},{1,5},{5,9},{9,13},{13,1},{2,6},{6,10},{... | collective-permute-start | bytes 49160 | tf_op jit(solution)/shard_map/ppermute | solution.py:18
  206.8 6.6 collective-permute-start.68
  208.0 5.4 collective-permute-start.69
  211.2 95.0 %collective-permute-start.64 = (f32[1,10,1,128]{3,2,1,0:T(1,128)S(1)}, f32[1,10,1,128]{3,2,1,0:T(1,128)S(1)}, u32[]{:S(2)}, u32[]{:S(2)}) collective-permute-start(f32[1,10,1,128]{3,2,1,0:T(1,128)S(1)} %get-tuple-element.248), channel_id=1, source_target_pairs={{1,0},{2,1},{3,2},{0,3},{5,4},{6,5},{7,6},{4,7},{9,8},{10,9},{11,1... | collective-permute-start | bytes 15368 | tf_op jit(solution)/shard_map/ppermute | solution.py:21
  211.3 94.9 %collective-permute-start.65 = (f32[1,10,1,128]{3,2,1,0:T(1,128)S(1)}, f32[1,10,1,128]{3,2,1,0:T(1,128)S(1)}, u32[]{:S(2)}, u32[]{:S(2)}) collective-permute-start(f32[1,10,1,128]{3,2,1,0:T(1,128)S(1)} %get-tuple-element.249), channel_id=1, source_target_pairs={{0,1},{1,2},{2,3},{3,0},{4,5},{5,6},{6,7},{7,4},{8,9},{9,10},{10,1... | collective-permute-start | bytes 15368 | tf_op jit(solution)/shard_map/ppermute | solution.py:18
  215.3 6.6 collective-permute-start.76
  217.4 5.0 collective-permute-start.77
  231.6 5.0 collective-permute-start.81
  311.2 5.2 collective-permute-start.85
  326.2 9.1 %collective-permute-start = (f32[1,8,8,128]{3,2,1,0:T(8,128)S(1)}, f32[1,8,8,128]{3,2,1,0:T(8,128)S(1)}, u32[]{:S(2)}, u32[]{:S(2)}) collective-permute-start(f32[1,8,8,128]{3,2,1,0:T(8,128)S(1)} %get-tuple-element.405), channel_id=1, source_target_pairs={{0,16},{16,32},{32,48},{48,64},{64,80},{80,96},{96,112},{1,17},{17... | collective-permute-start | bytes 98312 | tf_op jit(solution)/shard_map/while/body/eval_jaxpr/ppermute | solution.py:29
  376.9 7.9 %collective-permute-start = (f32[1,8,8,128]{3,2,1,0:T(8,128)S(1)}, f32[1,8,8,128]{3,2,1,0:T(8,128)S(1)}, u32[]{:S(2)}, u32[]{:S(2)}) collective-permute-start(f32[1,8,8,128]{3,2,1,0:T(8,128)S(1)} %get-tuple-element.405), channel_id=1, source_target_pairs={{0,16},{16,32},{32,48},{48,64},{64,80},{80,96},{96,112},{1,17},{17... | collective-permute-start | bytes 98312 | tf_op jit(solution)/shard_map/while/body/eval_jaxpr/ppermute | solution.py:29
  426.4 7.9 %collective-permute-start = (f32[1,8,8,128]{3,2,1,0:T(8,128)S(1)}, f32[1,8,8,128]{3,2,1,0:T(8,128)S(1)}, u32[]{:S(2)}, u32[]{:S(2)}) collective-permute-start(f32[1,8,8,128]{3,2,1,0:T(8,128)S(1)} %get-tuple-element.405), channel_id=1, source_target_pairs={{0,16},{16,32},{32,48},{48,64},{64,80},{80,96},{96,112},{1,17},{17... | collective-permute-start | bytes 98312 | tf_op jit(solution)/shard_map/while/body/eval_jaxpr/ppermute | solution.py:29
  475.9 7.9 %collective-permute-start = (f32[1,8,8,128]{3,2,1,0:T(8,128)S(1)}, f32[1,8,8,128]{3,2,1,0:T(8,128)S(1)}, u32[]{:S(2)}, u32[]{:S(2)}) collective-permute-start(f32[1,8,8,128]{3,2,1,0:T(8,128)S(1)} %get-tuple-element.405), channel_id=1, source_target_pairs={{0,16},{16,32},{32,48},{48,64},{64,80},{80,96},{96,112},{1,17},{17... | collective-permute-start | bytes 98312 | tf_op jit(solution)/shard_map/while/body/eval_jaxpr/ppermute | solution.py:29
  525.4 7.9 %collective-permute-start = (f32[1,8,8,128]{3,2,1,0:T(8,128)S(1)}, f32[1,8,8,128]{3,2,1,0:T(8,128)S(1)}, u32[]{:S(2)}, u32[]{:S(2)}) collective-permute-start(f32[1,8,8,128]{3,2,1,0:T(8,128)S(1)} %get-tuple-element.405), channel_id=1, source_target_pairs={{0,16},{16,32},{32,48},{48,64},{64,80},{80,96},{96,112},{1,17},{17... | collective-permute-start | bytes 98312 | tf_op jit(solution)/shard_map/while/body/eval_jaxpr/ppermute | solution.py:29
  574.9 7.9 %collective-permute-start = (f32[1,8,8,128]{3,2,1,0:T(8,128)S(1)}, f32[1,8,8,128]{3,2,1,0:T(8,128)S(1)}, u32[]{:S(2)}, u32[]{:S(2)}) collective-permute-start(f32[1,8,8,128]{3,2,1,0:T(8,128)S(1)} %get-tuple-element.405), channel_id=1, source_target_pairs={{0,16},{16,32},{32,48},{48,64},{64,80},{80,96},{96,112},{1,17},{17... | collective-permute-start | bytes 98312 | tf_op jit(solution)/shard_map/while/body/eval_jaxpr/ppermute | solution.py:29
  624.4 7.9 %collective-permute-start = (f32[1,8,8,128]{3,2,1,0:T(8,128)S(1)}, f32[1,8,8,128]{3,2,1,0:T(8,128)S(1)}, u32[]{:S(2)}, u32[]{:S(2)}) collective-permute-start(f32[1,8,8,128]{3,2,1,0:T(8,128)S(1)} %get-tuple-element.405), channel_id=1, source_target_pairs={{0,16},{16,32},{32,48},{48,64},{64,80},{80,96},{96,112},{1,17},{17... | collective-permute-start | bytes 98312 | tf_op jit(solution)/shard_map/while/body/eval_jaxpr/ppermute | solution.py:29
  (176 other events, 1196.6 us)
where the time goes:
time: 738 us; the launch traced here: 728 us
  waiting for transfers between devices  295 us (40%)
  starting transfers between devices  214 us (29%)
  local copies, waits for them, and re-layouts  168 us (23%)
  other arithmetic  49.7 us (7%)
    ppermute x92, waiting for transfers between devices, with_halo(): lax.ppermute(lax.slice_in_dim(block, block.shape[dim] - width, None, axis...  196 us
    ppermute x92, starting transfers between devices, with_halo(): lax.ppermute(lax.slice_in_dim(block, 0, width, axis=dim), axis, backward)  117 us
    reshape x2, local copies, waits for them, and re-layouts, restrict(): field.reshape(count, sx // 2, 2, sy // 2, 2, sz // 2, 2)  103 us
    ppermute x92, starting transfers between devices, with_halo(): lax.ppermute(lax.slice_in_dim(block, block.shape[dim] - width, None, axis...  78.7 us
    ppermute x92, waiting for transfers between devices, with_halo(): lax.ppermute(lax.slice_in_dim(block, 0, width, axis=dim), axis, backward)  57.4 us
    ppermute x8, waiting for transfers between devices, passed_along(): return lax.ppermute(value, axis, pairs)  41.5 us
    reshape x1, local copies, waits for them, and re-layouts, prolong(): return wide.reshape(count, sx * 2, sy * 2, sz * 2)  35.6 us
    reduce_sum x2, other arithmetic, restrict(): jnp.mean(field.reshape(count, sx // 2, 2, sy // 2, 2, sz // 2, 2), axis=(...  35.6 us
  transfers between devices with their start and end apart: 192, of which 169 were waited for; matrix products, arithmetic and copies ran while one was open for 12% of the time, Pallas kernels for 0%

commit v1 on v0

v1 whole, which is shorter than its diff:
```python
import jax
import jax.numpy as jnp
import numpy as np
from jax import lax
from jax.experimental import pallas as pl
from jax.experimental.pallas import tpu as pltpu
from jax.sharding import PartitionSpec as P

DT = 0.01
HALF = 0.005
W = ((5.0 / 24.0, 1.0 / 3.0, -1.0 / 24.0), (-1.0 / 24.0, 1.0 / 3.0, 5.0 / 24.0))
OLD = (
    (DT * (W[0][0] - 0.5), DT * W[0][1], DT * W[0][2]),
    (DT * W[1][0], DT * (W[1][1] - 0.5), DT * W[1][2]),
)
MESH = pl.DeviceIdType.MESH
DIRS = ((1, 0), (-1, 0), (0, 1), (0, -1), (1, 1), (1, -1), (-1, 1), (-1, -1))
F32 = jnp.float32
HIGH = lax.Precision.HIGHEST


def dot(a, b):
    return jnp.dot(a, b, precision=HIGH, preferred_element_type=F32)


def around(c, low, high):
    rows, z = c.shape
    s = (low + high) + (pltpu.roll(c, 1, 0) + pltpu.roll(c, rows - 1, 0))
    s = s + (pltpu.roll(c, 1, 1) + pltpu.roll(c, z - 1, 1))
    return s - 6.0 * c


def around3(v):
    c = v[1:-1]
    rows, z = c.shape[1:]
    s = v[:-2] + v[2:] + pltpu.roll(c, 1, 1) + pltpu.roll(c, rows - 1, 1)
    s = s + pltpu.roll(c, 1, 2) + pltpu.roll(c, z - 1, 2)
    return s - 6.0 * c


def loop(count, body, unroll=2):
    def step(i, carry):
        body(i)
        return carry

    lax.fori_loop(0, count, step, 0, unroll=unroll)


def potential(src, mu, count):
    def body(x):
        c = src[x + 1]
        mu[x] = c * (c * c - 1.0) - around(c, src[x], src[x + 2])

    loop(count, body)


def edge(h, d):
    return pl.ds(16 - h, h) if d > 0 else pl.ds(0, h)


def halo(h, d, at):
    return pl.ds(at - h, h) if d > 0 else pl.ds(at + 16, h)


def kernel(
    g, zavg, zdup, ydup, out,
    raw, rsy, rry, rrc, q, mu, mu2,
    start, k0, k1, ksy, kry, krc,
    u11, u12, u21, bb, usy, ury, urc, u22,
    fs, f11, f21, j0, j1,
    pair, co, cb, xext, gath, v0, v1, m0, stage, back, half,
    st_s, st_r, raw_s, raw_r, k_s, k_r, s_s, s_r, u_s, u_r, g_s, g_r, b_s, b_r,
):
    n, a, b = lax.axis_index("tm"), lax.axis_index("gx"), lax.axis_index("gy")

    def at(dt, dx, dy):
        return (lax.rem(n + dt + 8, 8), lax.rem(a + dx + 4, 4), lax.rem(b + dy + 4, 4))

    barrier = pltpu.get_barrier_semaphore()
    for dx, dy in DIRS:
        pl.semaphore_signal(barrier, inc=1, device_id=at(0, dx, dy), device_id_type=MESH)
    for dt in range(1, 8):
        pl.semaphore_signal(barrier, inc=1, device_id=at(dt, 0, 0), device_id_type=MESH)
    pl.semaphore_wait(barrier, 15)

    def send(src, dst, ss, rs, to):
        copy = pltpu.make_async_remote_copy(
            src_ref=src, dst_ref=dst, send_sem=ss, recv_sem=rs, device_id=to, device_id_type=MESH
        )
        copy.start()
        return copy

    mid = start.at[pl.ds(6, 16), pl.ds(8, 16), :]
    along = pltpu.make_async_remote_copy(
        src_ref=g.at[2, 0], dst_ref=mid, send_sem=st_s, recv_sem=st_r,
        device_id=at(1, 0, 0), device_id_type=MESH,
    )

    @pl.when(n < 7)
    def _():
        along.start()

    for j in range(3):
        rsy[0, :, 2 * j : 2 * j + 2, :] = g[j, 0, :, 14:16, :]
        rsy[1, :, 2 * j : 2 * j + 2, :] = g[j, 0, :, 0:2, :]
    raws = []
    for k, (dx, dy) in enumerate(DIRS):
        if dy == 0:
            src = g.at[:, 0, edge(2, dx)]
            dst = raw.at[:, halo(2, dx, 2), pl.ds(8, 16), :]
        elif dx == 0:
            src, dst = rsy.at[(1 - dy) // 2], rry.at[(1 - dy) // 2]
        else:
            src, dst = rsy.at[(1 - dy) // 2, edge(1, dx)], rrc.at[k - 4]
        raws.append(send(src, dst, raw_s.at[k], raw_r.at[k], at(0, dx, dy)))
    raw[:, 2:18, 8:24, :] = g[:, 0]
    for copy in raws:
        copy.wait_recv()
    for s, row in ((0, 6), (1, 24)):
        for j in range(3):
            raw[j, 2:18, row : row + 2, :] = rry[s, :, 2 * j : 2 * j + 2, :]
            for e, x in ((0, 1), (2, 18)):
                raw[j, x, row : row + 2, :] = rrc[e + s, 0, 2 * j : 2 * j + 2, :]

    def mix(x):
        u = [raw[j, x] for j in range(3)]
        for i in range(2):
            q[i, x] = OLD[i][0] * u[0] + OLD[i][1] * u[1] + OLD[i][2] * u[2]

    def mix_potential(x):
        u = [raw[j, x + 1] for j in range(3)]
        w = [c * (c * c - 1.0) for c in u]
        for i, m in ((0, mu), (1, mu2)):
            cube = OLD[i][0] * w[0] + OLD[i][1] * w[1] + OLD[i][2] * w[2]
            m[x] = cube - around(q[i, x + 1], q[i, x], q[i, x + 2])

    def mix_force(x):
        k0[x + 4] = around(mu[x + 1], mu[x], mu[x + 2])
        k1[x + 2] = around(mu2[x + 1], mu2[x], mu2[x + 2])

    loop(20, mix)
    loop(18, mix_potential)

    def wide_halo(p, r, ys, yr, cr, ss, rs):
        ys[0, :, 0:4, :] = p[4:20, 20:24, :]
        ys[0, :, 4:6, :] = r[2:18, 22:24, :]
        ys[1, :, 0:4, :] = p[4:20, 8:12, :]
        ys[1, :, 4:6, :] = r[2:18, 8:10, :]
        copies = []
        for k, (dx, dy) in enumerate(DIRS):
            to = at(0, dx, dy)
            if dy == 0:
                rows = pl.ds(8, 16)
                own = pl.ds(16, 4) if dx > 0 else pl.ds(4, 4)
                copies.append(
                    send(p.at[own, rows], p.at[halo(4, dx, 4), rows], ss.at[k], rs.at[k], to)
                )
                own = pl.ds(16, 2) if dx > 0 else pl.ds(2, 2)
                copies.append(
                    send(r.at[own, rows], r.at[halo(2, dx, 2), rows], ss.at[8 + k], rs.at[8 + k], to)
                )
            elif dx == 0:
                s = (1 - dy) // 2
                copies.append(send(ys.at[s], yr.at[s], ss.at[k], rs.at[k], to))
            else:
                s = (1 - dy) // 2
                copies.append(send(ys.at[s, edge(3, dx)], cr.at[k - 4], ss.at[k], rs.at[k], to))
        return copies

    def place(copies, p, r, yr, cr):
        for copy in copies:
            copy.wait_recv()
        for s, low, near in ((0, 4, 6), (1, 24, 24)):
            p[4:20, low : low + 4, :] = yr[s, :, 0:4, :]
            r[2:18, near : near + 2, :] = yr[s, :, 4:6, :]
            p[1:4, low : low + 4, :] = cr[s, :, 0:4, :]
            r[1, near : near + 2, :] = cr[s, 2, 4:6, :]
            p[20:23, low : low + 4, :] = cr[2 + s, :, 0:4, :]
            r[18, near : near + 2, :] = cr[2 + s, 0, 4:6, :]

    def mix_force_stored(x):
        rows = pl.ds(8, 16)
        k0[x + 4, rows, :] = around(mu[x + 1], mu[x], mu[x + 2])[8:24]
        k1[x + 2, rows, :] = around(mu2[x + 1], mu2[x], mu2[x + 2])[8:24]

    loop(16, mix_force_stored)
    ks = wide_halo(k0, k1, ksy, kry, krc, k_s, k_r)

    @pl.when(n == 0)
    def _():
        start[6:22, 8:24, :] = g[0, 0]

    @pl.when(n > 0)
    def _():
        along.wait_recv()

    starts = []
    for k, (dx, dy) in enumerate(DIRS):
        if dy == 0:
            width = 6
        else:
            width = 5
        if dx == 0:
            xs = xd = pl.ds(6, 16)
        else:
            xs = pl.ds(22 - width, width) if dx > 0 else pl.ds(6, width)
            xd = pl.ds(6 - width, width) if dx > 0 else pl.ds(22, width)
        if dy == 0:
            ys = yd = pl.ds(8, 16)
        else:
            ys = pl.ds(16, 8) if dy > 0 else pl.ds(8, 8)
            yd = pl.ds(0, 8) if dy > 0 else pl.ds(24, 8)
        starts.append(
            send(start.at[xs, ys], start.at[xd, yd], s_s.at[k], s_r.at[k], at(0, dx, dy))
        )
    place(ks, k0, k1, kry, krc)
    for copy in starts:
        copy.wait_recv()

    potential(start, mu, 26)

    def first(x):
        f = around(mu[x + 1], mu[x], mu[x + 2])
        fs[x] = f
        u11[x] = start[x + 2] + HALF * f + k0[x]

    loop(24, first)
    potential(u11, mu, 22)

    def second(x):
        f = around(mu[x + 1], mu[x], mu[x + 2])
        f11[x] = f
        u12[x] = u11[x + 2] + HALF * f + k1[x]

    loop(20, second)
    potential(u12, mu, 18)

    def third(x):
        f2 = around(mu[x + 1], mu[x], mu[x + 2])[8:24]
        f0 = fs[x + 4, 8:24, :]
        f1 = f11[x + 2, 8:24, :]
        rows = pl.ds(8, 16)
        u21[x + 4, rows, :] = start[x + 6, 8:24, :] + DT * (W[0][0] * f0 + W[0][1] * f1 + W[0][2] * f2)
        bb[x + 2, rows, :] = OLD[1][0] * f0 + OLD[1][1] * f1 + OLD[1][2] * f2

    loop(16, third)
    us = wide_halo(u21, bb, usy, ury, urc, u_s, u_r)

    def restrict(read, count, rows):
        both = [(read(2 * i) + read(2 * i + 1)) * 0.25 for i in range(count)]
        flat = jnp.concatenate(both, axis=0)
        pair[0 : count * rows, :] = dot(flat, zavg[...])
        total = count * rows // 2
        return pair[pl.ds(0, total, stride=2), :] + pair[pl.ds(1, total, stride=2), :]

    def coarse_force(values):
        v = values.reshape(12, 16, 128)
        c = v[1:-1]
        m = c * (c * c - 1.0) - 0.25 * around3(v)
        co[...] = 0.25 * around3(m)
        return co[:, 4:12, :].reshape(64, 128)

    c0 = restrict(lambda x: start[x + 2], 12, 32)
    g0 = coarse_force(c0)
    co[...] = c0.reshape(12, 16, 128)[2:10]
    cb[0] = co[:, 4:12, :].reshape(64, 128)

    place(us, u21, bb, ury, urc)
    potential(u21, mu, 22)

    def fourth(x):
        f = around(mu[x + 1], mu[x], mu[x + 2])
        f21[x] = f
        u22[x] = u21[x + 2] + HALF * f + bb[x]

    loop(20, fourth)
    potential(u22, mu, 18)

    def fifth(x):
        f2 = around(mu[x + 1], mu[x], mu[x + 2])[8:24]
        f0 = fs[x + 4, 8:24, :]
        f1 = f21[x + 2, 8:24, :]
        j0[x] = DT * (W[0][0] * f0 + W[0][1] * f1 + W[0][2] * f2)
        j1[x] = DT * (W[1][0] * f0 + W[1][1] * f1 + W[1][2] * f2)

    loop(16, fifth)
    c1 = restrict(lambda x: u21[x], 12, 32)
    g1 = coarse_force(c1)
    co[...] = c1.reshape(12, 16, 128)[2:10]
    cb[1] = co[:, 4:12, :].reshape(64, 128)
    cb[2] = restrict(lambda x: u22[x + 2, 8:24, :], 8, 16)
    part0 = restrict(lambda x: j0[x], 8, 16)
    part1 = restrict(lambda x: j1[x], 8, 16)
    part0 = part0 + jnp.where(n == 0, cb[0], -HALF * g0)
    part1 = part1 - HALF * g1
    turned = jnp.transpose(jnp.concatenate([part0, part1], axis=0))
    xext[32:160, :] = turned
    xext[0:32, :] = turned[96:128]
    xext[160:192, :] = turned[0:32]

    block = a * 4 + b
    is_chain = jnp.logical_and(lax.rem(a, 2) == 0, b == lax.rem(n + a, 4))
    mine = jnp.where(is_chain, n + 8 * (a // 2), -1)

    for c in range(4):
        length = 72 - 16 * c

        @pl.when(n // 2 == c)
        def _():
            def each(p):
                src = xext.at[pl.ds(pl.multiple_of(8 * p + 8 * c, 8), length), :]
                dst = gath.at[n, block, pl.ds(8 * c, length), :]
                t = lax.rem(p, 8)
                x = 2 * (p // 8)

                @pl.when(p != mine)
                def _():
                    send(src, dst, g_s, g_r.at[n], (t, x, lax.rem(t + x, 4)))

                @pl.when(p == mine)
                def _():
                    pltpu.make_async_copy(src, dst, g_r.at[n]).start()

            loop(16, each, 1)

    lane = lax.broadcasted_iota(jnp.int32, (72, 128), 1)

    def chain_lap(ref, t, rows):
        x, y = t // 4, lax.rem(t, 4)
        c = ref[t, rows, :]
        o = ref[(1 - x) * 4 + y, rows, :]
        up = ref[x * 4 + lax.rem(y + 1, 4), rows, :]
        down = ref[x * 4 + lax.rem(y + 3, 4), rows, :]
        size = c.shape[0]
        l = lane[:size]
        s = jnp.where(l < 120, pltpu.roll(c, 120, 1), pltpu.roll(o, 120, 1))
        s = s + jnp.where(l >= 8, pltpu.roll(c, 8, 1), pltpu.roll(o, 8, 1))
        inner = l & 7
        s = s + jnp.where(inner < 7, pltpu.roll(c, 127, 1), pltpu.roll(up, 7, 1))
        s = s + jnp.where(inner > 0, pltpu.roll(c, 1, 1), pltpu.roll(down, 121, 1))
        s = s + pltpu.roll(c, 1, 0) + pltpu.roll(c, size - 1, 0)
        return c, 0.25 * (s - 6.0 * c)

    @pl.when(is_chain)
    def _():
        me = n + 8 * (a // 2)
        v0[...] = jnp.zeros_like(v0)

        def sweep(src, dst, rows, m, first):
            def one(t):
                c, l = chain_lap(src, t, rows)
                m0[t, rows, :] = c * (c * c - 1.0) - l

            def two(t):
                _, f = chain_lap(m0, t, rows)
                x, y = t // 4, lax.rem(t, 4)
                e, o = gath[m, 8 * x + y, rows, :], gath[m, 8 * x + 4 + y, rows, :]
                l = lane[: e.shape[0]]
                if first:
                    part = jnp.where(l < 64, e, pltpu.roll(o, 64, 1))
                else:
                    part = jnp.where(l < 64, pltpu.roll(e, 64, 1), o)
                dst[t, rows, :] = src[t, rows, :] + HALF * f + part

            loop(8, one, 1)
            loop(8, two, 1)

        for c in range(4):
            rows = pl.ds(8 * c, 72 - 16 * c)

            def turn(i):
                m = 2 * c + i
                whole = gath.at[m, :, rows, :]
                pltpu.make_async_copy(whole, whole, g_r.at[m]).wait()
                stage[m, :, 0] = v0[:, 32:40, :]
                sweep(v0, v1, rows, m, True)
                stage[m, :, 1] = v1[:, 32:40, :]
                sweep(v1, v0, rows, m, False)
                stage[m, :, 2] = v0[:, 32:40, :]

                def each(d):
                    x, y = d // 4, lax.rem(d, 4)
                    src = stage.at[m, (x // 2) * 4 + y]
                    dst = back.at[:, pl.ds(pl.multiple_of(8 * me, 8), 8), :]
                    own = jnp.logical_and(m == n, d == block)

                    @pl.when(jnp.logical_not(own))
                    def _():
                        send(src, dst, b_s, b_r, (m, x, y))

                    @pl.when(own)
                    def _():
                        pltpu.make_async_copy(src, dst, b_r).start()

                loop(16, each, 1)

            loop(2, turn, 1)

    pltpu.make_async_copy(back, back, b_r).wait()
    for j in range(3):
        half[...] = jnp.transpose(back[j])
        rows = pl.ds(pl.multiple_of(64 * lax.rem(a, 2), 64), 64)
        change = half[rows, :] - cb[j]
        if j == 0:
            change = jnp.where(n == 0, 0.0, change)
        fine = dot(dot(ydup[...], change), zdup[...])
        for i in range(8):
            add = fine[16 * i : 16 * i + 16]
            for x in (2 * i, 2 * i + 1):
                if j == 0:
                    node = start[x + 6, 8:24, :]
                elif j == 1:
                    node = u21[x + 4, 8:24, :]
                else:
                    node = u22[x + 2, 8:24, :]
                out[j, 0, x] = node + add

    @pl.when(n < 7)
    def _():
        along.wait_send()

    for copy in raws + ks + starts + us:
        copy.wait_send()
    for c in range(4):
        length = 72 - 16 * c

        @pl.when(n // 2 == c)
        def _():
            @pl.when(is_chain)
            def _():
                sent = gath.at[0, 0:15, pl.ds(8 * c, length), :]
                pltpu.make_async_copy(sent, sent, g_s).wait()

            @pl.when(jnp.logical_not(is_chain))
            def _():
                sent = gath.at[0, :, pl.ds(8 * c, length), :]
                pltpu.make_async_copy(sent, sent, g_s).wait()

    @pl.when(is_chain)
    def _():
        for m in range(8):
            count = stage.at[m]
            if m == 0:
                count = stage.at[0, 0:7]
            pltpu.make_async_copy(count, count, b_s).wait()
        for m in range(8):
            pltpu.make_async_copy(stage.at[m], stage.at[m], b_s).wait()


def local(guess):
    zavg = np.zeros((256, 128), np.float32)
    zavg[np.arange(256), np.arange(256) // 2] = 0.5
    zdup = np.zeros((128, 256), np.float32)
    zdup[np.arange(256) // 2, np.arange(256)] = 1.0
    ydup = np.zeros((128, 64), np.float32)
    r = np.arange(128)
    ydup[r, (r // 16) * 8 + (r % 16) // 2] = 1.0
    vm = lambda *s: pltpu.VMEM(s, F32)
    dma = lambda *s: pltpu.SemaphoreType.DMA(s)
    vspec = pl.BlockSpec(memory_space=pltpu.VMEM)
    return pl.pallas_call(
        kernel,
        out_shape=jax.ShapeDtypeStruct(guess.shape, F32),
        in_specs=[vspec] * 4,
        out_specs=vspec,
        scratch_shapes=[
            vm(3, 20, 32, 256), vm(2, 16, 8, 256), vm(2, 16, 8, 256), vm(4, 1, 8, 256),
            vm(2, 20, 32, 256), vm(28, 32, 256), vm(28, 32, 256),
            vm(28, 32, 256), vm(24, 32, 256), vm(20, 32, 256),
            vm(2, 16, 8, 256), vm(2, 16, 8, 256), vm(4, 3, 8, 256),
            vm(24, 32, 256), vm(20, 32, 256), vm(24, 32, 256), vm(20, 32, 256),
            vm(2, 16, 8, 256), vm(2, 16, 8, 256), vm(4, 3, 8, 256), vm(20, 32, 256),
            vm(24, 32, 256), vm(20, 32, 256), vm(20, 32, 256), vm(16, 16, 256), vm(16, 16, 256),
            vm(384, 128), vm(8, 16, 128), vm(3, 64, 128), vm(192, 128),
            vm(8, 16, 72, 128), vm(8, 72, 128), vm(8, 72, 128), vm(8, 72, 128),
            vm(8, 8, 3, 8, 128), vm(3, 128, 128), vm(128, 128),
            pltpu.SemaphoreType.DMA, pltpu.SemaphoreType.DMA,
            dma(8), dma(8), dma(10), dma(10), dma(8), dma(8), dma(10), dma(10),
            pltpu.SemaphoreType.DMA, dma(8), pltpu.SemaphoreType.DMA, pltpu.SemaphoreType.DMA,
        ],
        compiler_params=pltpu.CompilerParams(
            collective_id=0, has_side_effects=True, vmem_limit_bytes=48 * 1024 * 1024
        ),
    )(guess, jnp.asarray(zavg), jnp.asarray(zdup), jnp.asarray(ydup))


def solution(mesh):
    spec = P(None, "tm", "gx", "gy", None)
    return jax.shard_map(local, mesh=mesh, in_specs=(spec,), out_specs=spec, check_vma=False)
```

time: 738 us -> 109 us (0.15)
  the two profiles are of different devices: /device:TPU:2 before, /device:TPU:27 now
where the time goes in v1:
time: 109 us
  Pallas kernels  105 us (96%)
  local copies, waits for them, and re-layouts  4.66 us (4%)
    pallas_call x1, Pallas kernels, local(): pl.pallas_call(kernel, out_shape=jax.ShapeDtypeStruct(guess.shape, F32),...  105 us
    unnamed x9, local copies, waits for them, and re-layouts  4.66 us

profile of v1, /device:TPU:27, one launch (start us, length us, event | category | flops | bytes accessed | tf_op | source)
XLA Modules:
  0.0 109.2 jit_solution(16163698038124692719)
XLA Ops:
  0.0 0.0 copy-start
  0.0 1.1 %copy-done = f32[3,1,16,16,256]{4,3,2,1,0:T(8,128)S(1)} copy-done((f32[3,1,16,16,256]{4,3,2,1,0:T(8,128)S(1)}, f32[3,1,16,16,256]{4,3,2,1,0:T(8,128)}, u32[]{:S(2)}) %copy-start) | copy-done | bytes 786456
  1.1 0.0 copy-start.1
  1.1 0.9 copy-done.1
  2.0 0.0 copy-start.2
  2.0 0.9 copy-done.2
  2.9 0.0 copy-start.3
  2.9 0.8 copy-done.3
  3.8 104.5 %shard_map.46 = f32[3,1,16,16,256]{4,3,2,1,0:T(8,128)S(1)} custom-call(f32[3,1,16,16,256]{4,3,2,1,0:T(8,128)S(1)} %copy-done, f32[256,128]{1,0:T(8,128)S(1)} %copy-done.2, f32[128,256]{1,0:T(8,128)S(1)} %copy-done.1, f32[128,64]{1,0:T(8,128)S(1)} %copy-done.3), custom_call_target="tpu_custom_call" | custom-call | tf_op jit(solution)/shard_map/pallas_call | solution.py:461
  108.3 0.9 copy.6
Async XLA Ops:
  0.0 1.1 %copy-start = (f32[3,1,16,16,256]{4,3,2,1,0:T(8,128)S(1)}, f32[3,1,16,16,256]{4,3,2,1,0:T(8,128)}, u32[]{:S(2)}) copy-start(f32[3,1,16,16,256]{4,3,2,1,0:T(8,128)} %g.1) | copy-start | bytes 2359300
  1.1 0.9 copy-start.1
  2.0 0.9 copy-start.2
  2.9 0.8 copy-start.3

commit v2 on v1

--- a/solution.py
+++ b/solution.py
@@ -1,6 +1,5 @@
 import jax
 import jax.numpy as jnp
-import numpy as np
 from jax import lax
 from jax.experimental import pallas as pl
 from jax.experimental.pallas import tpu as pltpu
@@ -63,13 +62,13 @@
 
 
 def kernel(
-    g, zavg, zdup, ydup, out,
-    raw, rsy, rry, rrc, q, mu, mu2,
+    g, out,
+    zavg, zdup, ydup, raw, rsy, rry, rrc, q, mu, mu2,
     start, k0, k1, ksy, kry, krc,
     u11, u12, u21, bb, usy, ury, urc, u22,
     fs, f11, f21, j0, j1,
     pair, co, cb, xext, gath, v0, v1, m0, stage, back, half,
-    st_s, st_r, raw_s, raw_r, k_s, k_r, s_s, s_r, u_s, u_r, g_s, g_r, b_s, b_r,
+    in_s, st_s, st_r, raw_s, raw_r, k_s, k_r, s_s, s_r, u_s, u_r, g_s, g_r, b_s, b_r,
 ):
     n, a, b = lax.axis_index("tm"), lax.axis_index("gx"), lax.axis_index("gy")
 
@@ -81,6 +80,24 @@
         pl.semaphore_signal(barrier, inc=1, device_id=at(0, dx, dy), device_id_type=MESH)
     for dt in range(1, 8):
         pl.semaphore_signal(barrier, inc=1, device_id=at(dt, 0, 0), device_id_type=MESH)
+
+    block16 = (pl.ds(2, 16), pl.ds(8, 16))
+    loads = [pltpu.make_async_copy(g.at[j, 0], raw.at[j, *block16], in_s.at[j]) for j in range(3)]
+    for load in loads:
+        load.start()
+
+    def iota(shape, d):
+        return lax.broadcasted_iota(jnp.int32, shape, d)
+
+    zavg[...] = jnp.where(iota((256, 128), 0) // 2 == iota((256, 128), 1), 0.5, 0.0)
+    zdup[...] = jnp.where(iota((128, 256), 0) == iota((128, 256), 1) // 2, 1.0, 0.0)
+    r, k = iota((128, 64), 0), iota((128, 64), 1)
+    ydup[...] = jnp.where(k == (r // 16) * 8 + lax.rem(r, 16) // 2, 1.0, 0.0)
+    for load in loads:
+        load.wait()
+    for j in range(3):
+        rsy[0, :, 2 * j : 2 * j + 2, :] = raw[j, 2:18, 22:24, :]
+        rsy[1, :, 2 * j : 2 * j + 2, :] = raw[j, 2:18, 8:10, :]
     pl.semaphore_wait(barrier, 15)
 
     def send(src, dst, ss, rs, to):
@@ -92,7 +109,7 @@
 
     mid = start.at[pl.ds(6, 16), pl.ds(8, 16), :]
     along = pltpu.make_async_remote_copy(
-        src_ref=g.at[2, 0], dst_ref=mid, send_sem=st_s, recv_sem=st_r,
+        src_ref=raw.at[2, *block16], dst_ref=mid, send_sem=st_s, recv_sem=st_r,
         device_id=at(1, 0, 0), device_id_type=MESH,
     )
 
@@ -100,20 +117,43 @@
     def _():
         along.start()
 
-    for j in range(3):
-        rsy[0, :, 2 * j : 2 * j + 2, :] = g[j, 0, :, 14:16, :]
-        rsy[1, :, 2 * j : 2 * j + 2, :] = g[j, 0, :, 0:2, :]
     raws = []
     for k, (dx, dy) in enumerate(DIRS):
         if dy == 0:
-            src = g.at[:, 0, edge(2, dx)]
+            src = raw.at[:, pl.ds(16, 2) if dx > 0 else pl.ds(2, 2), pl.ds(8, 16), :]
             dst = raw.at[:, halo(2, dx, 2), pl.ds(8, 16), :]
         elif dx == 0:
             src, dst = rsy.at[(1 - dy) // 2], rry.at[(1 - dy) // 2]
         else:
             src, dst = rsy.at[(1 - dy) // 2, edge(1, dx)], rrc.at[k - 4]
         raws.append(send(src, dst, raw_s.at[k], raw_r.at[k], at(0, dx, dy)))
-    raw[:, 2:18, 8:24, :] = g[:, 0]
+    @pl.when(n == 0)
+    def _():
+        start[6:22, 8:24, :] = raw[0, 2:18, 8:24, :]
+
+    @pl.when(n > 0)
+    def _():
+        along.wait_recv()
+
+    starts = []
+    for k, (dx, dy) in enumerate(DIRS):
+        if dy == 0:
+            width = 6
+        else:
+            width = 5
+        if dx == 0:
+            xs = xd = pl.ds(6, 16)
+        else:
+            xs = pl.ds(22 - width, width) if dx > 0 else pl.ds(6, width)
+            xd = pl.ds(6 - width, width) if dx > 0 else pl.ds(22, width)
+        if dy == 0:
+            ys = yd = pl.ds(8, 16)
+        else:
+            ys = pl.ds(16, 8) if dy > 0 else pl.ds(8, 8)
+            yd = pl.ds(0, 8) if dy > 0 else pl.ds(24, 8)
+        starts.append(
+            send(start.at[xs, ys], start.at[xd, yd], s_s.at[k], s_r.at[k], at(0, dx, dy))
+        )
     for copy in raws:
         copy.wait_recv()
     for s, row in ((0, 6), (1, 24)):
@@ -133,10 +173,6 @@
         for i, m in ((0, mu), (1, mu2)):
             cube = OLD[i][0] * w[0] + OLD[i][1] * w[1] + OLD[i][2] * w[2]
             m[x] = cube - around(q[i, x + 1], q[i, x], q[i, x + 2])
-
-    def mix_force(x):
-        k0[x + 4] = around(mu[x + 1], mu[x], mu[x + 2])
-        k1[x + 2] = around(mu2[x + 1], mu2[x], mu2[x + 2])
 
     loop(20, mix)
     loop(18, mix_potential)
@@ -186,33 +222,6 @@
     loop(16, mix_force_stored)
     ks = wide_halo(k0, k1, ksy, kry, krc, k_s, k_r)
 
-    @pl.when(n == 0)
-    def _():
-        start[6:22, 8:24, :] = g[0, 0]
-
-    @pl.when(n > 0)
-    def _():
-        along.wait_recv()
-
-    starts = []
-    for k, (dx, dy) in enumerate(DIRS):
-        if dy == 0:
-            width = 6
-        else:
-            width = 5
-        if dx == 0:
-            xs = xd = pl.ds(6, 16)
-        else:
-            xs = pl.ds(22 - width, width) if dx > 0 else pl.ds(6, width)
-            xd = pl.ds(6 - width, width) if dx > 0 else pl.ds(22, width)
-        if dy == 0:
-            ys = yd = pl.ds(8, 16)
-        else:
-            ys = pl.ds(16, 8) if dy > 0 else pl.ds(8, 8)
-            yd = pl.ds(0, 8) if dy > 0 else pl.ds(24, 8)
-        starts.append(
-            send(start.at[xs, ys], start.at[xd, yd], s_s.at[k], s_r.at[k], at(0, dx, dy))
-        )
     place(ks, k0, k1, kry, krc)
     for copy in starts:
         copy.wait_recv()
@@ -323,47 +332,44 @@
 
             loop(16, each, 1)
 
-    lane = lax.broadcasted_iota(jnp.int32, (72, 128), 1)
-
-    def chain_lap(ref, t, rows):
-        x, y = t // 4, lax.rem(t, 4)
-        c = ref[t, rows, :]
-        o = ref[(1 - x) * 4 + y, rows, :]
-        up = ref[x * 4 + lax.rem(y + 1, 4), rows, :]
-        down = ref[x * 4 + lax.rem(y + 3, 4), rows, :]
-        size = c.shape[0]
-        l = lane[:size]
-        s = jnp.where(l < 120, pltpu.roll(c, 120, 1), pltpu.roll(o, 120, 1))
-        s = s + jnp.where(l >= 8, pltpu.roll(c, 8, 1), pltpu.roll(o, 8, 1))
-        inner = l & 7
-        s = s + jnp.where(inner < 7, pltpu.roll(c, 127, 1), pltpu.roll(up, 7, 1))
-        s = s + jnp.where(inner > 0, pltpu.roll(c, 1, 1), pltpu.roll(down, 121, 1))
-        s = s + pltpu.roll(c, 1, 0) + pltpu.roll(c, size - 1, 0)
-        return c, 0.25 * (s - 6.0 * c)
+    lane = lax.broadcasted_iota(jnp.int32, (8, 128), 1)
+    inner = lane & 7
+
+    def chain_lap(ref, lo, hi, put):
+        for r in range(lo, hi, 8):
+            c = [ref[t, r : r + 8, :] for t in range(8)]
+            turn = lambda by: [pltpu.roll(v, by % 128, 1) for v in c]
+            xp, xm, yp, ym, yu, yd = (turn(by) for by in (-8, 8, -1, 1, 7, -7))
+            for t in range(8):
+                o, up, down = (t + 4) % 8, t // 4 * 4 + (t + 1) % 4, t // 4 * 4 + (t + 3) % 4
+                s = jnp.where(lane < 120, xp[t], xp[o]) + jnp.where(lane >= 8, xm[t], xm[o])
+                s = s + (jnp.where(inner < 7, yp[t], yu[up]) + jnp.where(inner > 0, ym[t], yd[down]))
+                s = s + (ref[t, r + 1 : r + 9, :] + ref[t, r - 1 : r + 7, :])
+                put(t, r, c[t], 0.25 * (s - 6.0 * c[t]))
 
     @pl.when(is_chain)
     def _():
         me = n + 8 * (a // 2)
         v0[...] = jnp.zeros_like(v0)
 
-        def sweep(src, dst, rows, m, first):
-            def one(t):
-                c, l = chain_lap(src, t, rows)
-                m0[t, rows, :] = c * (c * c - 1.0) - l
-
-            def two(t):
-                _, f = chain_lap(m0, t, rows)
-                x, y = t // 4, lax.rem(t, 4)
+        def sweep(src, dst, c, m, first):
+            lo, hi = 8 + 8 * c, 80 - 8 * c
+
+            def one(t, r, u, l):
+                m0[t, r : r + 8, :] = u * (u * u - 1.0) - l
+
+            def two(t, r, u, f):
+                x, y = t // 4, t % 4
+                rows = pl.ds(r - 8, 8)
                 e, o = gath[m, 8 * x + y, rows, :], gath[m, 8 * x + 4 + y, rows, :]
-                l = lane[: e.shape[0]]
                 if first:
-                    part = jnp.where(l < 64, e, pltpu.roll(o, 64, 1))
+                    part = jnp.where(lane < 64, e, pltpu.roll(o, 64, 1))
                 else:
-                    part = jnp.where(l < 64, pltpu.roll(e, 64, 1), o)
-                dst[t, rows, :] = src[t, rows, :] + HALF * f + part
-
-            loop(8, one, 1)
-            loop(8, two, 1)
+                    part = jnp.where(lane < 64, pltpu.roll(e, 64, 1), o)
+                dst[t, r : r + 8, :] = src[t, r : r + 8, :] + HALF * f + part
+
+            chain_lap(src, lo, hi, one)
+            chain_lap(m0, lo, hi, two)
 
         for c in range(4):
             rows = pl.ds(8 * c, 72 - 16 * c)
@@ -372,11 +378,11 @@
                 m = 2 * c + i
                 whole = gath.at[m, :, rows, :]
                 pltpu.make_async_copy(whole, whole, g_r.at[m]).wait()
-                stage[m, :, 0] = v0[:, 32:40, :]
-                sweep(v0, v1, rows, m, True)
-                stage[m, :, 1] = v1[:, 32:40, :]
-                sweep(v1, v0, rows, m, False)
-                stage[m, :, 2] = v0[:, 32:40, :]
+                stage[m, :, 0] = v0[:, 40:48, :]
+                sweep(v0, v1, c, m, True)
+                stage[m, :, 1] = v1[:, 40:48, :]
+                sweep(v1, v0, c, m, False)
+                stage[m, :, 2] = v0[:, 40:48, :]
 
                 def each(d):
                     x, y = d // 4, lax.rem(d, 4)
@@ -448,22 +454,16 @@
 
 
 def local(guess):
-    zavg = np.zeros((256, 128), np.float32)
-    zavg[np.arange(256), np.arange(256) // 2] = 0.5
-    zdup = np.zeros((128, 256), np.float32)
-    zdup[np.arange(256) // 2, np.arange(256)] = 1.0
-    ydup = np.zeros((128, 64), np.float32)
-    r = np.arange(128)
-    ydup[r, (r // 16) * 8 + (r % 16) // 2] = 1.0
     vm = lambda *s: pltpu.VMEM(s, F32)
     dma = lambda *s: pltpu.SemaphoreType.DMA(s)
     vspec = pl.BlockSpec(memory_space=pltpu.VMEM)
     return pl.pallas_call(
         kernel,
         out_shape=jax.ShapeDtypeStruct(guess.shape, F32),
-        in_specs=[vspec] * 4,
+        in_specs=[pl.BlockSpec(memory_space=pl.ANY)],
         out_specs=vspec,
         scratch_shapes=[
+            vm(256, 128), vm(128, 256), vm(128, 64),
             vm(3, 20, 32, 256), vm(2, 16, 8, 256), vm(2, 16, 8, 256), vm(4, 1, 8, 256),
             vm(2, 20, 32, 256), vm(28, 32, 256), vm(28, 32, 256),
             vm(28, 32, 256), vm(24, 32, 256), vm(20, 32, 256),
@@ -472,16 +472,16 @@
             vm(2, 16, 8, 256), vm(2, 16, 8, 256), vm(4, 3, 8, 256), vm(20, 32, 256),
             vm(24, 32, 256), vm(20, 32, 256), vm(20, 32, 256), vm(16, 16, 256), vm(16, 16, 256),
             vm(384, 128), vm(8, 16, 128), vm(3, 64, 128), vm(192, 128),
-            vm(8, 16, 72, 128), vm(8, 72, 128), vm(8, 72, 128), vm(8, 72, 128),
+            vm(8, 16, 72, 128), vm(8, 88, 128), vm(8, 88, 128), vm(8, 88, 128),
             vm(8, 8, 3, 8, 128), vm(3, 128, 128), vm(128, 128),
-            pltpu.SemaphoreType.DMA, pltpu.SemaphoreType.DMA,
+            dma(3), pltpu.SemaphoreType.DMA, pltpu.SemaphoreType.DMA,
             dma(8), dma(8), dma(10), dma(10), dma(8), dma(8), dma(10), dma(10),
             pltpu.SemaphoreType.DMA, dma(8), pltpu.SemaphoreType.DMA, pltpu.SemaphoreType.DMA,
         ],
         compiler_params=pltpu.CompilerParams(
             collective_id=0, has_side_effects=True, vmem_limit_bytes=48 * 1024 * 1024
         ),
-    )(guess, jnp.asarray(zavg), jnp.asarray(zdup), jnp.asarray(ydup))
+    )(guess)
 
 
 def solution(mesh):

time: 109 us -> 83.1 us (0.76)
  Pallas kernels: 105 us -> 80.9 us
  local copies, waits for them, and re-layouts: 4.66 us -> 2.01 us
    pallas_call x1, Pallas kernels: 105 us -> 80.9 us  [local(): pl.pallas_call(kernel, out_shape=jax.ShapeDtypeStruct(guess.shape, F32),...]
    unnamed x9 -> x3, local copies, waits for them, and re-layouts: 4.66 us -> 2.01 us
where the time goes in v2:
time: 83.1 us; the launch traced here: 82.9 us
  Pallas kernels  80.9 us (97%)
  local copies, waits for them, and re-layouts  2.01 us (2%)
    pallas_call x1, Pallas kernels, local(): pl.pallas_call(kernel, out_shape=jax.ShapeDtypeStruct(guess.shape, F32),...  80.9 us
    unnamed x3, local copies, waits for them, and re-layouts  2.01 us

profile of v2, /device:TPU:27, one launch (start us, length us, event | category | flops | bytes accessed | tf_op | source)
XLA Modules:
  0.0 82.9 jit_solution(3309755041980554496)
XLA Ops:
  0.0 0.0 copy-start
  0.0 1.1 %copy-done = f32[3,1,16,16,256]{4,3,2,1,0:T(8,128)S(1)} copy-done((f32[3,1,16,16,256]{4,3,2,1,0:T(8,128)S(1)}, f32[3,1,16,16,256]{4,3,2,1,0:T(8,128)}, u32[]{:S(2)}) %copy-start) | copy-done | bytes 786456
  1.1 80.9 %shard_map.17 = f32[3,1,16,16,256]{4,3,2,1,0:T(8,128)S(1)} custom-call(f32[3,1,16,16,256]{4,3,2,1,0:T(8,128)S(1)} %copy-done), custom_call_target="tpu_custom_call" | custom-call | tf_op jit(solution)/shard_map/pallas_call | solution.py:460
  82.0 0.9 %copy.3 = f32[3,1,16,16,256]{4,3,2,1,0:T(8,128)} copy(f32[3,1,16,16,256]{4,3,2,1,0:T(8,128)S(1)} %shard_map.17) | data formatting | bytes 1572864
Async XLA Ops:
  0.0 1.1 %copy-start = (f32[3,1,16,16,256]{4,3,2,1,0:T(8,128)S(1)}, f32[3,1,16,16,256]{4,3,2,1,0:T(8,128)}, u32[]{:S(2)}) copy-start(f32[3,1,16,16,256]{4,3,2,1,0:T(8,128)} %g.1) | copy-start | bytes 2359300

commit v3 on v2

v3 whole, which is shorter than its diff:
```python
import jax
import jax.numpy as jnp
from jax import lax
from jax.experimental import pallas as pl
from jax.experimental.pallas import tpu as pltpu
from jax.sharding import PartitionSpec as P

DT = 0.01
HALF = 0.005
W = ((5.0 / 24.0, 1.0 / 3.0, -1.0 / 24.0), (-1.0 / 24.0, 1.0 / 3.0, 5.0 / 24.0))
OLD = (
    (DT * (W[0][0] - 0.5), DT * W[0][1], DT * W[0][2]),
    (DT * W[1][0], DT * (W[1][1] - 0.5), DT * W[1][2]),
)
MESH = pl.DeviceIdType.MESH
DIRS = ((1, 0), (-1, 0), (0, 1), (0, -1), (1, 1), (1, -1), (-1, 1), (-1, -1))
F32 = jnp.float32
HIGH = lax.Precision.HIGHEST


def dot(a, b):
    return jnp.dot(a, b, precision=HIGH, preferred_element_type=F32)


def around(c, low, high):
    rows, z = c.shape
    s = (low + high) + (pltpu.roll(c, 1, 0) + pltpu.roll(c, rows - 1, 0))
    s = s + (pltpu.roll(c, 1, 1) + pltpu.roll(c, z - 1, 1))
    return s - 6.0 * c


def around3(v):
    c = v[1:-1]
    rows, z = c.shape[1:]
    s = v[:-2] + v[2:] + pltpu.roll(c, 1, 1) + pltpu.roll(c, rows - 1, 1)
    s = s + pltpu.roll(c, 1, 2) + pltpu.roll(c, z - 1, 2)
    return s - 6.0 * c


def loop(count, body, group=1):
    def step(i, carry):
        base = jnp.minimum(group * i, count - group)
        for k in range(group):
            body(base + k)
        return carry

    lax.fori_loop(0, -(-count // group), step, 0)


def potential(src, mu, count, group):
    def body(x):
        c = src[x + 1]
        mu[x] = c * (c * c - 1.0) - around(c, src[x], src[x + 2])

    loop(count, body, group)


def crop(v):
    return pltpu.roll(v, 28, 0)[0:24]


def edge(h, d):
    return pl.ds(16 - h, h) if d > 0 else pl.ds(0, h)


def halo(h, d, at):
    return pl.ds(at - h, h) if d > 0 else pl.ds(at + 16, h)


def kernel(
    g, out,
    zavg, zdup, ydup, raw, rsy, rry, rrc, q, w, mu, mu2,
    start, k0, k1, ksx, krx, ksy, kry, krc,
    u11, u12, u21, bb, usx, urx, usy, ury, urc, u22,
    fs, f11, f21, j0, j1, wide,
    pair, co, cb, xext, gath, v0, v1, m0, seam, stage, back, half,
    in_s, st_s, st_r, raw_s, raw_r, k_s, k_r, s_s, s_r, u_s, u_r, g_s, g_r, x_s, x_r, b_s, b_r,
):
    n, a, b = lax.axis_index("tm"), lax.axis_index("gx"), lax.axis_index("gy")

    def at(dt, dx, dy):
        return (lax.rem(n + dt + 8, 8), lax.rem(a + dx + 4, 4), lax.rem(b + dy + 4, 4))

    barrier = pltpu.get_barrier_semaphore()
    for dx, dy in DIRS:
        pl.semaphore_signal(barrier, inc=1, device_id=at(0, dx, dy), device_id_type=MESH)
    for dt in range(1, 8):
        pl.semaphore_signal(barrier, inc=1, device_id=at(dt, 0, 0), device_id_type=MESH)

    block16 = (pl.ds(2, 16), pl.ds(8, 16))
    loads = [pltpu.make_async_copy(g.at[j, 0], raw.at[j, *block16], in_s.at[j]) for j in range(3)]
    for load in loads:
        load.start()

    def iota(shape, d):
        return lax.broadcasted_iota(jnp.int32, shape, d)

    zavg[...] = jnp.where(iota((256, 128), 0) // 2 == iota((256, 128), 1), 0.5, 0.0)
    zdup[...] = jnp.where(iota((128, 256), 0) == iota((128, 256), 1) // 2, 1.0, 0.0)
    r, k = iota((128, 64), 0), iota((128, 64), 1)
    ydup[...] = jnp.where(k == (r // 16) * 8 + lax.rem(r, 16) // 2, 1.0, 0.0)
    for load in loads:
        load.wait()
    for j in range(3):
        rsy[0, :, 2 * j : 2 * j + 2, :] = raw[j, 2:18, 22:24, :]
        rsy[1, :, 2 * j : 2 * j + 2, :] = raw[j, 2:18, 8:10, :]
    pl.semaphore_wait(barrier, 15)

    def send(src, dst, ss, rs, to):
        copy = pltpu.make_async_remote_copy(
            src_ref=src, dst_ref=dst, send_sem=ss, recv_sem=rs, device_id=to, device_id_type=MESH
        )
        copy.start()
        return copy

    mid = start.at[pl.ds(6, 16), pl.ds(8, 16), :]
    along = pltpu.make_async_remote_copy(
        src_ref=raw.at[2, *block16], dst_ref=mid, send_sem=st_s, recv_sem=st_r,
        device_id=at(1, 0, 0), device_id_type=MESH,
    )

    @pl.when(n < 7)
    def _():
        along.start()

    raws = []
    for k, (dx, dy) in enumerate(DIRS):
        if dy == 0:
            src = raw.at[:, pl.ds(16, 2) if dx > 0 else pl.ds(2, 2), pl.ds(8, 16), :]
            dst = raw.at[:, halo(2, dx, 2), pl.ds(8, 16), :]
        elif dx == 0:
            src, dst = rsy.at[(1 - dy) // 2], rry.at[(1 - dy) // 2]
        else:
            src, dst = rsy.at[(1 - dy) // 2, edge(1, dx)], rrc.at[k - 4]
        raws.append(send(src, dst, raw_s.at[k], raw_r.at[k], at(0, dx, dy)))
    @pl.when(n == 0)
    def _():
        start[6:22, 8:24, :] = raw[0, 2:18, 8:24, :]

    @pl.when(n > 0)
    def _():
        along.wait_recv()

    starts = []
    for k, (dx, dy) in enumerate(DIRS):
        if dy == 0:
            width = 6
        else:
            width = 5
        if dx == 0:
            xs = xd = pl.ds(6, 16)
        else:
            xs = pl.ds(22 - width, width) if dx > 0 else pl.ds(6, width)
            xd = pl.ds(6 - width, width) if dx > 0 else pl.ds(22, width)
        if dy == 0:
            ys = yd = pl.ds(8, 16)
        else:
            ys = pl.ds(16, 8) if dy > 0 else pl.ds(8, 8)
            yd = pl.ds(0, 8) if dy > 0 else pl.ds(24, 8)
        starts.append(
            send(start.at[xs, ys], start.at[xd, yd], s_s.at[k], s_r.at[k], at(0, dx, dy))
        )
    for copy in raws:
        copy.wait_recv()
    for s, row in ((0, 6), (1, 24)):
        for j in range(3):
            raw[j, 2:18, row : row + 2, :] = rry[s, :, 2 * j : 2 * j + 2, :]
            for e, x in ((0, 1), (2, 18)):
                raw[j, x, row : row + 2, :] = rrc[e + s, 0, 2 * j : 2 * j + 2, :]

    def mix(x):
        u = [raw[j, x] for j in range(3)]
        c = [v * (v * v - 1.0) for v in u]
        for i in range(2):
            q[i, x] = crop(OLD[i][0] * u[0] + OLD[i][1] * u[1] + OLD[i][2] * u[2])
            w[i, x] = crop(OLD[i][0] * c[0] + OLD[i][1] * c[1] + OLD[i][2] * c[2])

    def mix_potential(x):
        for i, m in ((0, mu), (1, mu2)):
            m[x] = w[i, x + 1] - around(q[i, x + 1], q[i, x], q[i, x + 2])

    def mix_force(x):
        k0[x + 4, 4:20, :] = around(mu[x + 1], mu[x], mu[x + 2])[4:20]
        k1[x + 2, 4:20, :] = around(mu2[x + 1], mu2[x], mu2[x + 2])[4:20]

    loop(20, mix, 5)
    loop(18, mix_potential, 6)
    loop(16, mix_force, 4)

    def wide_halo(p, r, xs, xr, ys, yr, cr, ss, rs):
        ys[0, :, 0:4, :] = p[4:20, 16:20, :]
        ys[0, :, 4:6, :] = r[2:18, 18:20, :]
        ys[1, :, 0:4, :] = p[4:20, 4:8, :]
        ys[1, :, 4:6, :] = r[2:18, 4:6, :]
        xs[0, 0:4] = p[16:20, 4:20, :]
        xs[0, 4:6] = r[16:18, 4:20, :]
        xs[1, 0:4] = p[4:8, 4:20, :]
        xs[1, 4:6] = r[2:4, 4:20, :]
        copies = []
        for k, (dx, dy) in enumerate(DIRS):
            s = (1 - dy) // 2
            if dy == 0:
                src, dst = xs.at[(1 - dx) // 2], xr.at[(1 - dx) // 2]
            elif dx == 0:
                src, dst = ys.at[s], yr.at[s]
            else:
                src, dst = ys.at[s, edge(3, dx)], cr.at[k - 4]
            copies.append(send(src, dst, ss.at[k], rs.at[k], at(0, dx, dy)))
        return copies

    def place(copies, p, r, xr, yr, cr):
        for copy in copies:
            copy.wait_recv()
        p[0:4, 4:20, :] = xr[0, 0:4]
        r[0:2, 4:20, :] = xr[0, 4:6]
        p[20:24, 4:20, :] = xr[1, 0:4]
        r[18:20, 4:20, :] = xr[1, 4:6]
        for s, low, near in ((0, 0, 2), (1, 20, 20)):
            p[4:20, low : low + 4, :] = yr[s, :, 0:4, :]
            r[2:18, near : near + 2, :] = yr[s, :, 4:6, :]
            p[1:4, low : low + 4, :] = cr[s, :, 0:4, :]
            r[1, near : near + 2, :] = cr[s, 2, 4:6, :]
            p[20:23, low : low + 4, :] = cr[2 + s, :, 0:4, :]
            r[18, near : near + 2, :] = cr[2 + s, 0, 4:6, :]

    ks = wide_halo(k0, k1, ksx, krx, ksy, kry, krc, k_s, k_r)

    for copy in starts:
        copy.wait_recv()
    potential(start, wide, 26, 9)
    place(ks, k0, k1, krx, kry, krc)

    def first(x):
        f = around(wide[x + 1], wide[x], wide[x + 2])
        fs[x] = crop(f)
        u11[x] = crop(start[x + 2] + HALF * f) + k0[x]

    loop(24, first, 8)
    potential(u11, mu, 22, 8)

    def second(x):
        f = around(mu[x + 1], mu[x], mu[x + 2])
        f11[x] = f
        u12[x] = u11[x + 2] + HALF * f + k1[x]

    loop(20, second, 10)
    potential(u12, mu, 18, 9)

    def third(x):
        f2 = around(mu[x + 1], mu[x], mu[x + 2])
        f0, f1 = fs[x + 4], f11[x + 2]
        new = crop(start[x + 6]) + DT * (W[0][0] * f0 + W[0][1] * f1 + W[0][2] * f2)
        u21[x + 4, 4:20, :] = new[4:20]
        bb[x + 2, 4:20, :] = (OLD[1][0] * f0 + OLD[1][1] * f1 + OLD[1][2] * f2)[4:20]

    loop(16, third, 8)
    us = wide_halo(u21, bb, usx, urx, usy, ury, urc, u_s, u_r)

    def average(layers, rows):
        both = [(layers[2 * i] + layers[2 * i + 1]) * 0.25 for i in range(len(layers) // 2)]
        pair[0 : len(both) * rows, :] = dot(jnp.concatenate(both, axis=0), zavg[...])

    def coarse_rows(first_row, count):
        return pair[pl.ds(first_row, count, stride=2), :] + pair[pl.ds(first_row + 1, count, stride=2), :]

    def bricks(rows, offset, skip):
        return jnp.concatenate([coarse_rows(rows * (i + skip) + offset, 8) for i in range(8)], axis=0)

    def coarse_force(rows, offset):
        v = jnp.concatenate([coarse_rows(rows * i + offset, 16) for i in range(12)], axis=0)
        v = v.reshape(12, 16, 128)
        c = v[1:-1]
        m = c * (c * c - 1.0) - 0.25 * around3(v)
        co[...] = 0.25 * around3(m)
        return jnp.concatenate([co[i, 2:10, :] for i in range(8)], axis=0)

    average([start[x + 2] for x in range(24)], 32)
    cb[0] = bricks(32, 8, 2)
    g0 = coarse_force(32, 4)
    place(us, u21, bb, urx, ury, urc)
    potential(u21, mu, 22, 8)

    def fourth(x):
        f = around(mu[x + 1], mu[x], mu[x + 2])
        f21[x] = f
        u22[x] = u21[x + 2] + HALF * f + bb[x]

    loop(20, fourth, 10)
    potential(u22, mu, 18, 9)

    def fifth(x):
        f2 = around(mu[x + 1], mu[x], mu[x + 2])
        f0, f1 = fs[x + 4], f21[x + 2]
        j0[x] = DT * (W[0][0] * f0 + W[0][1] * f1 + W[0][2] * f2)
        j1[x] = DT * (W[1][0] * f0 + W[1][1] * f1 + W[1][2] * f2)

    loop(16, fifth, 8)
    average([u21[x] for x in range(24)], 24)
    cb[1] = bricks(24, 4, 2)
    g1 = coarse_force(24, 0)
    average([u22[x + 2] for x in range(16)], 24)
    cb[2] = bricks(24, 4, 0)
    average([j0[x] for x in range(16)], 24)
    part0 = bricks(24, 4, 0)
    average([j1[x] for x in range(16)], 24)
    part1 = bricks(24, 4, 0)
    part0 = part0 + jnp.where(n == 0, cb[0], -HALF * g0)
    part1 = part1 - HALF * g1
    turned = jnp.transpose(jnp.concatenate([part0, part1], axis=0))
    xext[32:160, :] = turned
    xext[0:32, :] = turned[96:128]
    xext[160:192, :] = turned[0:32]

    block = a * 4 + b

    def chain_device(p):
        t, x = lax.rem(p, 8), 2 * (p // 8)
        return (t, x, lax.rem(x + t // 4 + t, 4))

    is_chain = jnp.logical_and(lax.rem(a, 2) == 0, b == lax.rem(a + n // 4 + n, 4))
    me = n + 8 * (a // 2)
    mine = jnp.where(is_chain, me, -1)
    late = lax.rem(n, 4) // 2

    for c, (low, length) in enumerate(((0, 40), (8, 24))):

        @pl.when(late == c)
        def _():
            def each(p):
                src = xext.at[pl.ds(pl.multiple_of(8 * p + 16 + low, 8), length), :]
                dst = gath.at[n, block, pl.ds(low, length), :]

                @pl.when(p != mine)
                def _():
                    send(src, dst, g_s, g_r.at[n], chain_device(p))

                @pl.when(p == mine)
                def _():
                    pltpu.make_async_copy(src, dst, g_r.at[n]).start()

            loop(16, each)

    lane = lax.broadcasted_iota(jnp.int32, (8, 128), 1)
    inner = lane & 7

    def chain_lap(ref, lo, hi, put):
        for r in range(lo, hi, 8):
            c = [ref[t, r : r + 8, :] for t in range(8)]
            turn = lambda by: [pltpu.roll(v, by % 128, 1) for v in c]
            xp, xm, yp, ym, yu, yd = (turn(by) for by in (-8, 8, -1, 1, 7, -7))
            for t in range(8):
                o, up, down = (t + 4) % 8, t // 4 * 4 + (t + 1) % 4, t // 4 * 4 + (t + 3) % 4
                s = jnp.where(lane < 120, xp[t], xp[o]) + jnp.where(lane >= 8, xm[t], xm[o])
                s = s + (jnp.where(inner < 7, yp[t], yu[up]) + jnp.where(inner > 0, ym[t], yd[down]))
                s = s + (ref[t, r + 1 : r + 9, :] + ref[t, r - 1 : r + 7, :])
                put(t, r, c[t], 0.25 * (s - 6.0 * c[t]))

    @pl.when(is_chain)
    def _():
        v0[...] = jnp.zeros_like(v0)

        def sweep(src, dst, m, first, inside, outside):
            def one(t, r, u, l):
                m0[t, r : r + 8, :] = u * (u * u - 1.0) - l

            def two(t, r, u, f):
                x, y = t // 4, t % 4
                rows = pl.ds(r - 8, 8)
                e, o = gath[m, 8 * x + y, rows, :], gath[m, 8 * x + 4 + y, rows, :]
                if first:
                    part = jnp.where(lane < 64, e, pltpu.roll(o, 64, 1))
                else:
                    part = jnp.where(lane < 64, pltpu.roll(e, 64, 1), o)
                dst[t, r : r + 8, :] = src[t, r : r + 8, :] + HALF * f + part

            chain_lap(src, *inside, one)
            chain_lap(m0, *outside, two)

        full, part, core = (8, 48), (16, 40), (24, 32)
        spans = (
            (full, full, full, full),
            (full, full, full, part),
            (part, part, part, part),
            (part, part, part, core),
        )

        def other(d, k):
            p = lax.rem(me + d + 16, 16)
            return pltpu.make_async_remote_copy(
                src_ref=stage.at[3, :, 2], dst_ref=seam.at[k], send_sem=x_s.at[k], recv_sem=x_r.at[k],
                device_id=chain_device(p), device_id_type=MESH,
            )

        seams = [other(d, k) for k, d in ((0, 2), (1, 1), (3, -1), (4, -2))]

        def scatter(m):
            def each(d):
                x, y = d // 4, lax.rem(d, 4)
                src = stage.at[m, (x // 2) * 4 + y]
                dst = back.at[:, pl.ds(pl.multiple_of(8 * me, 8), 8), :]
                own = jnp.logical_and(m == n, d == block)

                @pl.when(jnp.logical_not(own))
                def _():
                    send(src, dst, b_s, b_r, (m, x, y))

                @pl.when(own)
                def _():
                    pltpu.make_async_copy(src, dst, b_r).start()

            loop(16, each)

        def phase(h):
            @pl.when(h == 1)
            def _():
                for copy in seams:
                    copy.start()
                for m in range(4):
                    scatter(m)
                for copy in seams:
                    copy.wait()
                for k in (0, 1, 3, 4):
                    v0[:, 8 + 8 * k : 16 + 8 * k, :] = seam[k]

            for i in range(4):
                m = 4 * h + i
                low, length = ((0, 40), (8, 24))[i // 2]
                whole = gath.at[m, :, pl.ds(low, length), :]
                pltpu.make_async_copy(whole, whole, g_r.at[m]).wait()
                stage[m, :, 0] = v0[:, 24:32, :]
                sweep(v0, v1, m, True, *spans[i][:2])
                stage[m, :, 1] = v1[:, 24:32, :]
                sweep(v1, v0, m, False, *spans[i][2:])
                stage[m, :, 2] = v0[:, 24:32, :]

                @pl.when(h == 1)
                def _():
                    scatter(m)

        loop(2, phase)

    pltpu.make_async_copy(back, back, b_r).wait()
    for j in range(3):
        half[...] = jnp.transpose(back[j])
        rows = pl.ds(pl.multiple_of(64 * lax.rem(a, 2), 64), 64)
        change = half[rows, :] - cb[j]
        if j == 0:
            change = jnp.where(n == 0, 0.0, change)
        fine = dot(dot(ydup[...], change), zdup[...])
        for i in range(8):
            add = fine[16 * i : 16 * i + 16]
            for x in (2 * i, 2 * i + 1):
                if j == 0:
                    node = start[x + 6, 8:24, :]
                elif j == 1:
                    node = u21[x + 4, 4:20, :]
                else:
                    node = u22[x + 2, 4:20, :]
                out[j, 0, x] = node + add

    @pl.when(n < 7)
    def _():
        along.wait_send()

    for copy in raws + ks + starts + us:
        copy.wait_send()
    for c, (low, length) in enumerate(((0, 40), (8, 24))):

        @pl.when(late == c)
        def _():
            @pl.when(is_chain)
            def _():
                sent = gath.at[0, 0:15, pl.ds(low, length), :]
                pltpu.make_async_copy(sent, sent, g_s).wait()

            @pl.when(jnp.logical_not(is_chain))
            def _():
                sent = gath.at[0, :, pl.ds(low, length), :]
                pltpu.make_async_copy(sent, sent, g_s).wait()

    @pl.when(is_chain)
    def _():
        for m in range(8):
            count = stage.at[m]
            if m == 0:
                count = stage.at[0, 0:7]
            pltpu.make_async_copy(count, count, b_s).wait()
        for m in range(8):
            pltpu.make_async_copy(stage.at[m], stage.at[m], b_s).wait()


def local(guess):
    vm = lambda *s: pltpu.VMEM(s, F32)
    dma = lambda *s: pltpu.SemaphoreType.DMA(s)
    vspec = pl.BlockSpec(memory_space=pltpu.VMEM)
    return pl.pallas_call(
        kernel,
        out_shape=jax.ShapeDtypeStruct(guess.shape, F32),
        in_specs=[pl.BlockSpec(memory_space=pl.ANY)],
        out_specs=vspec,
        scratch_shapes=[
            vm(256, 128), vm(128, 256), vm(128, 64),
            vm(3, 20, 32, 256), vm(2, 16, 8, 256), vm(2, 16, 8, 256), vm(4, 1, 8, 256),
            vm(2, 20, 24, 256), vm(2, 20, 24, 256), vm(22, 24, 256), vm(22, 24, 256),
            vm(28, 32, 256), vm(24, 24, 256), vm(20, 24, 256),
            vm(2, 6, 16, 256), vm(2, 6, 16, 256), vm(2, 16, 8, 256), vm(2, 16, 8, 256), vm(4, 3, 8, 256),
            vm(24, 24, 256), vm(20, 24, 256), vm(24, 24, 256), vm(20, 24, 256),
            vm(2, 6, 16, 256), vm(2, 6, 16, 256), vm(2, 16, 8, 256), vm(2, 16, 8, 256), vm(4, 3, 8, 256),
            vm(20, 24, 256),
            vm(24, 24, 256), vm(20, 24, 256), vm(20, 24, 256), vm(16, 24, 256), vm(16, 24, 256), vm(26, 32, 256),
            vm(400, 128), vm(8, 16, 128), vm(3, 64, 128), vm(192, 128),
            vm(8, 16, 40, 128), vm(8, 56, 128), vm(8, 56, 128), vm(8, 56, 128), vm(5, 8, 8, 128),
            vm(8, 8, 3, 8, 128), vm(3, 128, 128), vm(128, 128),
            dma(3), pltpu.SemaphoreType.DMA, pltpu.SemaphoreType.DMA,
            dma(8), dma(8), dma(8), dma(8), dma(8), dma(8), dma(8), dma(8),
            pltpu.SemaphoreType.DMA, dma(8), dma(5), dma(5),
            pltpu.SemaphoreType.DMA, pltpu.SemaphoreType.DMA,
        ],
        compiler_params=pltpu.CompilerParams(
            collective_id=0, has_side_effects=True, vmem_limit_bytes=48 * 1024 * 1024
        ),
    )(guess)


def solution(mesh):
    spec = P(None, "tm", "gx", "gy", None)
    return jax.shard_map(local, mesh=mesh, in_specs=(spec,), out_specs=spec, check_vma=False)
```

time: 83.1 us -> 71.1 us (0.86)
  Pallas kernels: 80.9 us -> 69 us
    pallas_call x1, Pallas kernels: 80.9 us -> 69 us  [local(): pl.pallas_call(kernel, out_shape=jax.ShapeDtypeStruct(guess.shape, F32),...]
where the time goes in v3:
time: 71.1 us; the launch traced here: 71 us
  Pallas kernels  69 us (97%)
  local copies, waits for them, and re-layouts  2.01 us (3%)
    pallas_call x1, Pallas kernels, local(): pl.pallas_call(kernel, out_shape=jax.ShapeDtypeStruct(guess.shape, F32),...  69 us
    unnamed x3, local copies, waits for them, and re-layouts  2.01 us

profile of v3, /device:TPU:27, one launch (start us, length us, event | category | flops | bytes accessed | tf_op | source)
XLA Modules:
  0.0 71.0 jit_solution(15410356028255423946)
XLA Ops:
  0.0 0.0 copy-start
  0.0 1.1 %copy-done = f32[3,1,16,16,256]{4,3,2,1,0:T(8,128)S(1)} copy-done((f32[3,1,16,16,256]{4,3,2,1,0:T(8,128)S(1)}, f32[3,1,16,16,256]{4,3,2,1,0:T(8,128)}, u32[]{:S(2)}) %copy-start) | copy-done | bytes 786456
  1.1 69.0 %shard_map.17 = f32[3,1,16,16,256]{4,3,2,1,0:T(8,128)S(1)} custom-call(f32[3,1,16,16,256]{4,3,2,1,0:T(8,128)S(1)} %copy-done), custom_call_target="tpu_custom_call" | custom-call | tf_op jit(solution)/shard_map/pallas_call | solution.py:496
  70.1 0.9 %copy.3 = f32[3,1,16,16,256]{4,3,2,1,0:T(8,128)} copy(f32[3,1,16,16,256]{4,3,2,1,0:T(8,128)S(1)} %shard_map.17) | data formatting | bytes 1572864
Async XLA Ops:
  0.0 1.1 %copy-start = (f32[3,1,16,16,256]{4,3,2,1,0:T(8,128)S(1)}, f32[3,1,16,16,256]{4,3,2,1,0:T(8,128)}, u32[]{:S(2)}) copy-start(f32[3,1,16,16,256]{4,3,2,1,0:T(8,128)} %g.1) | copy-start | bytes 2359300

commit v4 on v3

--- a/solution.py
+++ b/solution.py
@@ -67,11 +67,30 @@
     return pl.ds(at - h, h) if d > 0 else pl.ds(at + 16, h)
 
 
+CORNER = ((1, 0, 5), (4, 5, 2), (2, 8, 4), (3, 12, 3), (5, 15, 1))
+
+
+def pack_corner(field, packed, k):
+    dx, dy = DIRS[4 + k]
+    for d, row, count in CORNER:
+        x = 22 - d if dx > 0 else 5 + d
+        y = 24 - count if dy > 0 else 8
+        packed[..., k, row : row + count, :] = field[..., x, y : y + count, :]
+
+
+def unpack_corner(field, packed, k):
+    dx, dy = DIRS[4 + k]
+    for d, row, count in CORNER:
+        x = 6 - d if dx > 0 else 21 + d
+        y = 8 - count if dy > 0 else 24
+        field[..., x, y : y + count, :] = packed[..., k, row : row + count, :]
+
+
 def kernel(
     g, out,
     zavg, zdup, ydup, raw, rsy, rry, rrc, q, w, mu, mu2,
-    start, k0, k1, ksx, krx, ksy, kry, krc,
-    u11, u12, u21, bb, usx, urx, usy, ury, urc, u22,
+    start, ssc, src_c, k0, k1, ksx, krx, ksy, kry, ksc, krc,
+    u11, u12, u21, bb, usx, urx, usy, ury, usc, urc, u22,
     fs, f11, f21, j0, j1, wide,
     pair, co, cb, xext, gath, v0, v1, m0, seam, stage, back, half,
     in_s, st_s, st_r, raw_s, raw_r, k_s, k_r, s_s, s_r, u_s, u_r, g_s, g_r, x_s, x_r, b_s, b_r,
@@ -141,25 +160,23 @@
     def _():
         along.wait_recv()
 
+    for k in range(4):
+        pack_corner(start, ssc, k)
     starts = []
     for k, (dx, dy) in enumerate(DIRS):
-        if dy == 0:
-            width = 6
-        else:
-            width = 5
         if dx == 0:
             xs = xd = pl.ds(6, 16)
         else:
-            xs = pl.ds(22 - width, width) if dx > 0 else pl.ds(6, width)
-            xd = pl.ds(6 - width, width) if dx > 0 else pl.ds(22, width)
+            xs, xd = (pl.ds(16, 6), pl.ds(0, 6)) if dx > 0 else (pl.ds(6, 6), pl.ds(22, 6))
         if dy == 0:
             ys = yd = pl.ds(8, 16)
         else:
-            ys = pl.ds(16, 8) if dy > 0 else pl.ds(8, 8)
-            yd = pl.ds(0, 8) if dy > 0 else pl.ds(24, 8)
-        starts.append(
-            send(start.at[xs, ys], start.at[xd, yd], s_s.at[k], s_r.at[k], at(0, dx, dy))
-        )
+            ys, yd = (pl.ds(16, 8), pl.ds(0, 8)) if dy > 0 else (pl.ds(8, 8), pl.ds(24, 8))
+        if k < 4:
+            src, dst = start.at[xs, ys], start.at[xd, yd]
+        else:
+            src, dst = ssc.at[k - 4], src_c.at[k - 4]
+        starts.append(send(src, dst, s_s.at[k], s_r.at[k], at(0, dx, dy)))
     for copy in raws:
         copy.wait_recv()
     for s, row in ((0, 6), (1, 24)):
@@ -187,7 +204,7 @@
     loop(18, mix_potential, 6)
     loop(16, mix_force, 4)
 
-    def wide_halo(p, r, xs, xr, ys, yr, cr, ss, rs):
+    def wide_halo(p, r, xs, xr, ys, yr, cs, cr, ss, rs):
         ys[0, :, 0:4, :] = p[4:20, 16:20, :]
         ys[0, :, 4:6, :] = r[2:18, 18:20, :]
         ys[1, :, 0:4, :] = p[4:20, 4:8, :]
@@ -196,6 +213,12 @@
         xs[0, 4:6] = r[16:18, 4:20, :]
         xs[1, 0:4] = p[4:8, 4:20, :]
         xs[1, 4:6] = r[2:4, 4:20, :]
+        for k, (dx, dy) in enumerate(DIRS[4:]):
+            for row, d, count in ((0, 1, 3), (3, 2, 2), (5, 3, 1)):
+                x = 20 - d if dx > 0 else 3 + d
+                y = 20 - count if dy > 0 else 4
+                cs[k, row : row + count, :] = p[x, y : y + count, :]
+            cs[k, 6:7, :] = r[17 if dx > 0 else 2, pl.ds(19 if dy > 0 else 4, 1), :]
         copies = []
         for k, (dx, dy) in enumerate(DIRS):
             s = (1 - dy) // 2
@@ -204,7 +227,7 @@
             elif dx == 0:
                 src, dst = ys.at[s], yr.at[s]
             else:
-                src, dst = ys.at[s, edge(3, dx)], cr.at[k - 4]
+                src, dst = cs.at[k - 4], cr.at[k - 4]
             copies.append(send(src, dst, ss.at[k], rs.at[k], at(0, dx, dy)))
         return copies
 
@@ -218,15 +241,19 @@
         for s, low, near in ((0, 0, 2), (1, 20, 20)):
             p[4:20, low : low + 4, :] = yr[s, :, 0:4, :]
             r[2:18, near : near + 2, :] = yr[s, :, 4:6, :]
-            p[1:4, low : low + 4, :] = cr[s, :, 0:4, :]
-            r[1, near : near + 2, :] = cr[s, 2, 4:6, :]
-            p[20:23, low : low + 4, :] = cr[2 + s, :, 0:4, :]
-            r[18, near : near + 2, :] = cr[2 + s, 0, 4:6, :]
-
-    ks = wide_halo(k0, k1, ksx, krx, ksy, kry, krc, k_s, k_r)
+        for k, (dx, dy) in enumerate(DIRS[4:]):
+            for row, d, count in ((0, 1, 3), (3, 2, 2), (5, 3, 1)):
+                x = 4 - d if dx > 0 else 19 + d
+                y = 4 - count if dy > 0 else 20
+                p[x, y : y + count, :] = cr[k, row : row + count, :]
+            r[1 if dx > 0 else 18, pl.ds(3 if dy > 0 else 20, 1), :] = cr[k, 6:7, :]
+
+    ks = wide_halo(k0, k1, ksx, krx, ksy, kry, ksc, krc, k_s, k_r)
 
     for copy in starts:
         copy.wait_recv()
+    for k in range(4):
+        unpack_corner(start, src_c, k)
     potential(start, wide, 26, 9)
     place(ks, k0, k1, krx, kry, krc)
 
@@ -254,7 +281,7 @@
         bb[x + 2, 4:20, :] = (OLD[1][0] * f0 + OLD[1][1] * f1 + OLD[1][2] * f2)[4:20]
 
     loop(16, third, 8)
-    us = wide_halo(u21, bb, usx, urx, usy, ury, urc, u_s, u_r)
+    us = wide_halo(u21, bb, usx, urx, usy, ury, usc, urc, u_s, u_r)
 
     def average(layers, rows):
         both = [(layers[2 * i] + layers[2 * i + 1]) * 0.25 for i in range(len(layers) // 2)]
@@ -326,19 +353,19 @@
 
         @pl.when(late == c)
         def _():
-            def each(p):
+            def part(p):
                 src = xext.at[pl.ds(pl.multiple_of(8 * p + 16 + low, 8), length), :]
-                dst = gath.at[n, block, pl.ds(low, length), :]
+                return src, gath.at[n, block, pl.ds(low, length), :]
+
+            for p in range(16):
 
                 @pl.when(p != mine)
                 def _():
-                    send(src, dst, g_s, g_r.at[n], chain_device(p))
-
-                @pl.when(p == mine)
-                def _():
-                    pltpu.make_async_copy(src, dst, g_r.at[n]).start()
-
-            loop(16, each)
+                    send(*part(p), g_s, g_r.at[n], chain_device(p))
+
+            @pl.when(is_chain)
+            def _():
+                pltpu.make_async_copy(*part(me), g_r.at[n]).start()
 
     lane = lax.broadcasted_iota(jnp.int32, (8, 128), 1)
     inner = lane & 7
@@ -394,21 +421,22 @@
         seams = [other(d, k) for k, d in ((0, 2), (1, 1), (3, -1), (4, -2))]
 
         def scatter(m):
-            def each(d):
-                x, y = d // 4, lax.rem(d, 4)
+            for d in range(16):
+                to = lax.rem(block + d, 16)
+                x, y = to // 4, lax.rem(to, 4)
                 src = stage.at[m, (x // 2) * 4 + y]
                 dst = back.at[:, pl.ds(pl.multiple_of(8 * me, 8), 8), :]
-                own = jnp.logical_and(m == n, d == block)
-
-                @pl.when(jnp.logical_not(own))
-                def _():
+                if d > 0:
                     send(src, dst, b_s, b_r, (m, x, y))
-
-                @pl.when(own)
-                def _():
-                    pltpu.make_async_copy(src, dst, b_r).start()
-
-            loop(16, each)
+                else:
+
+                    @pl.when(m != n)
+                    def _():
+                        send(src, dst, b_s, b_r, (m, x, y))
+
+                    @pl.when(m == n)
+                    def _():
+                        pltpu.make_async_copy(src, dst, b_r).start()
 
         def phase(h):
             @pl.when(h == 1)
@@ -502,10 +530,10 @@
             vm(256, 128), vm(128, 256), vm(128, 64),
             vm(3, 20, 32, 256), vm(2, 16, 8, 256), vm(2, 16, 8, 256), vm(4, 1, 8, 256),
             vm(2, 20, 24, 256), vm(2, 20, 24, 256), vm(22, 24, 256), vm(22, 24, 256),
-            vm(28, 32, 256), vm(24, 24, 256), vm(20, 24, 256),
-            vm(2, 6, 16, 256), vm(2, 6, 16, 256), vm(2, 16, 8, 256), vm(2, 16, 8, 256), vm(4, 3, 8, 256),
+            vm(28, 32, 256), vm(4, 16, 256), vm(4, 16, 256), vm(24, 24, 256), vm(20, 24, 256),
+            vm(2, 6, 16, 256), vm(2, 6, 16, 256), vm(2, 16, 8, 256), vm(2, 16, 8, 256), vm(4, 8, 256), vm(4, 8, 256),
             vm(24, 24, 256), vm(20, 24, 256), vm(24, 24, 256), vm(20, 24, 256),
-            vm(2, 6, 16, 256), vm(2, 6, 16, 256), vm(2, 16, 8, 256), vm(2, 16, 8, 256), vm(4, 3, 8, 256),
+            vm(2, 6, 16, 256), vm(2, 6, 16, 256), vm(2, 16, 8, 256), vm(2, 16, 8, 256), vm(4, 8, 256), vm(4, 8, 256),
             vm(20, 24, 256),
             vm(24, 24, 256), vm(20, 24, 256), vm(20, 24, 256), vm(16, 24, 256), vm(16, 24, 256), vm(26, 32, 256),
             vm(400, 128), vm(8, 16, 128), vm(3, 64, 128), vm(192, 128),

time: 71.1 us -> 68.6 us (0.965)
  Pallas kernels: 69 us -> 66.4 us
    pallas_call x1, Pallas kernels: 69 us -> 66.4 us  [local(): pl.pallas_call(kernel, out_shape=jax.ShapeDtypeStruct(guess.shape, F32),...]
where the time goes in v4:
time: 68.6 us; the launch traced here: 68.4 us
  Pallas kernels  66.4 us (97%)
  local copies, waits for them, and re-layouts  2.01 us (3%)
    pallas_call x1, Pallas kernels, local(): pl.pallas_call(kernel, out_shape=jax.ShapeDtypeStruct(guess.shape, F32),...  66.4 us
    unnamed x3, local copies, waits for them, and re-layouts  2.01 us

profile of v4, /device:TPU:27, one launch (start us, length us, event | category | flops | bytes accessed | tf_op | source)
XLA Modules:
  0.0 68.4 jit_solution(5346142247141223667)
XLA Ops:
  0.0 0.0 copy-start
  0.0 1.1 %copy-done = f32[3,1,16,16,256]{4,3,2,1,0:T(8,128)S(1)} copy-done((f32[3,1,16,16,256]{4,3,2,1,0:T(8,128)S(1)}, f32[3,1,16,16,256]{4,3,2,1,0:T(8,128)}, u32[]{:S(2)}) %copy-start) | copy-done | bytes 786456
  1.1 66.4 %shard_map.17 = f32[3,1,16,16,256]{4,3,2,1,0:T(8,128)S(1)} custom-call(f32[3,1,16,16,256]{4,3,2,1,0:T(8,128)S(1)} %copy-done), custom_call_target="tpu_custom_call" | custom-call | tf_op jit(solution)/shard_map/pallas_call | solution.py:524
  67.5 0.9 %copy.3 = f32[3,1,16,16,256]{4,3,2,1,0:T(8,128)} copy(f32[3,1,16,16,256]{4,3,2,1,0:T(8,128)S(1)} %shard_map.17) | data formatting | bytes 1572864
Async XLA Ops:
  0.0 1.1 %copy-start = (f32[3,1,16,16,256]{4,3,2,1,0:T(8,128)S(1)}, f32[3,1,16,16,256]{4,3,2,1,0:T(8,128)}, u32[]{:S(2)}) copy-start(f32[3,1,16,16,256]{4,3,2,1,0:T(8,128)} %g.1) | copy-start | bytes 2359300

commit v5 on v4

--- a/solution.py
+++ b/solution.py
@@ -132,15 +132,19 @@
         copy.start()
         return copy
 
-    mid = start.at[pl.ds(6, 16), pl.ds(8, 16), :]
-    along = pltpu.make_async_remote_copy(
-        src_ref=raw.at[2, *block16], dst_ref=mid, send_sem=st_s, recv_sem=st_r,
-        device_id=at(1, 0, 0), device_id_type=MESH,
-    )
+    along = [
+        pltpu.make_async_remote_copy(
+            src_ref=raw.at[2, pl.ds(2 + 8 * h, 8), pl.ds(8, 16)],
+            dst_ref=start.at[pl.ds(6 + 8 * h, 8), pl.ds(8, 16)],
+            send_sem=st_s.at[h], recv_sem=st_r.at[h], device_id=at(1, 0, 0), device_id_type=MESH,
+        )
+        for h in range(2)
+    ]
 
     @pl.when(n < 7)
     def _():
-        along.start()
+        for copy in along:
+            copy.start()
 
     raws = []
     for k, (dx, dy) in enumerate(DIRS):
@@ -156,27 +160,28 @@
     def _():
         start[6:22, 8:24, :] = raw[0, 2:18, 8:24, :]
 
-    @pl.when(n > 0)
-    def _():
-        along.wait_recv()
-
-    for k in range(4):
-        pack_corner(start, ssc, k)
     starts = []
-    for k, (dx, dy) in enumerate(DIRS):
-        if dx == 0:
-            xs = xd = pl.ds(6, 16)
-        else:
-            xs, xd = (pl.ds(16, 6), pl.ds(0, 6)) if dx > 0 else (pl.ds(6, 6), pl.ds(22, 6))
-        if dy == 0:
-            ys = yd = pl.ds(8, 16)
-        else:
-            ys, yd = (pl.ds(16, 8), pl.ds(0, 8)) if dy > 0 else (pl.ds(8, 8), pl.ds(24, 8))
-        if k < 4:
-            src, dst = start.at[xs, ys], start.at[xd, yd]
-        else:
-            src, dst = ssc.at[k - 4], src_c.at[k - 4]
-        starts.append(send(src, dst, s_s.at[k], s_r.at[k], at(0, dx, dy)))
+    for h in range(2):
+
+        @pl.when(n > 0)
+        def _():
+            along[h].wait_recv()
+
+        layers = pl.ds(6 + 8 * h, 8)
+        for k, (dx, dy) in enumerate(DIRS):
+            if dx == (1, -1)[h]:
+                continue
+            to, slot = at(0, dx, dy), k + 10 * h if dx == 0 else k
+            if dx == 0:
+                ys, yd = (pl.ds(16, 8), pl.ds(0, 8)) if dy > 0 else (pl.ds(8, 8), pl.ds(24, 8))
+                src, dst = start.at[layers, ys], start.at[layers, yd]
+            elif dy == 0:
+                xs, xd = (pl.ds(16, 6), pl.ds(0, 6)) if dx > 0 else (pl.ds(6, 6), pl.ds(22, 6))
+                src, dst = start.at[xs, pl.ds(8, 16)], start.at[xd, pl.ds(8, 16)]
+            else:
+                pack_corner(start, ssc, k - 4)
+                src, dst = ssc.at[k - 4], src_c.at[k - 4]
+            starts.append(send(src, dst, s_s.at[slot], s_r.at[slot], to))
     for copy in raws:
         copy.wait_recv()
     for s, row in ((0, 6), (1, 24)):
@@ -414,7 +419,7 @@
         def other(d, k):
             p = lax.rem(me + d + 16, 16)
             return pltpu.make_async_remote_copy(
-                src_ref=stage.at[3, :, 2], dst_ref=seam.at[k], send_sem=x_s.at[k], recv_sem=x_r.at[k],
+                src_ref=stage.at[3, 0, :, 1], dst_ref=seam.at[k], send_sem=x_s.at[k], recv_sem=x_r.at[k],
                 device_id=chain_device(p), device_id_type=MESH,
             )
 
@@ -424,7 +429,7 @@
             for d in range(16):
                 to = lax.rem(block + d, 16)
                 x, y = to // 4, lax.rem(to, 4)
-                src = stage.at[m, (x // 2) * 4 + y]
+                src = stage.at[m, lax.rem(x, 2), (x // 2) * 4 + y]
                 dst = back.at[:, pl.ds(pl.multiple_of(8 * me, 8), 8), :]
                 if d > 0:
                     send(src, dst, b_s, b_r, (m, x, y))
@@ -443,8 +448,7 @@
             def _():
                 for copy in seams:
                     copy.start()
-                for m in range(4):
-                    scatter(m)
+                scatter(3)
                 for copy in seams:
                     copy.wait()
                 for k in (0, 1, 3, 4):
@@ -455,23 +459,32 @@
                 low, length = ((0, 40), (8, 24))[i // 2]
                 whole = gath.at[m, :, pl.ds(low, length), :]
                 pltpu.make_async_copy(whole, whole, g_r.at[m]).wait()
-                stage[m, :, 0] = v0[:, 24:32, :]
+                begin = [v0[t, 24:32, :] for t in range(8)]
                 sweep(v0, v1, m, True, *spans[i][:2])
-                stage[m, :, 1] = v1[:, 24:32, :]
+                for t in range(8):
+                    middle = v1[t, 24:32, :]
+                    stage[m, 0, t, 0] = jnp.where(lane < 64, begin[t], pltpu.roll(middle, 64, 1))
+                    stage[m, 1, t, 0] = jnp.where(lane < 64, pltpu.roll(begin[t], 64, 1), middle)
                 sweep(v1, v0, m, False, *spans[i][2:])
-                stage[m, :, 2] = v0[:, 24:32, :]
-
-                @pl.when(h == 1)
-                def _():
+                stage[m, 0, :, 1] = v0[:, 24:32, :]
+                stage[m, 1, :, 1] = v0[:, 24:32, :]
+
+                if i < 3:
                     scatter(m)
+                else:
+
+                    @pl.when(h == 1)
+                    def _():
+                        scatter(m)
 
         loop(2, phase)
 
     pltpu.make_async_copy(back, back, b_r).wait()
+    half[0] = jnp.transpose(back[0])
+    half[1] = jnp.transpose(back[1])
+    own_half = pl.ds(pl.multiple_of(64 * lax.rem(a, 2), 64), 64)
     for j in range(3):
-        half[...] = jnp.transpose(back[j])
-        rows = pl.ds(pl.multiple_of(64 * lax.rem(a, 2), 64), 64)
-        change = half[rows, :] - cb[j]
+        change = (half[0, 0:64], half[0, 64:128], half[1, own_half])[j] - cb[j]
         if j == 0:
             change = jnp.where(n == 0, 0.0, change)
         fine = dot(dot(ydup[...], change), zdup[...])
@@ -488,7 +501,8 @@
 
     @pl.when(n < 7)
     def _():
-        along.wait_send()
+        for copy in along:
+            copy.wait_send()
 
     for copy in raws + ks + starts + us:
         copy.wait_send()
@@ -508,12 +522,11 @@
 
     @pl.when(is_chain)
     def _():
-        for m in range(8):
-            count = stage.at[m]
-            if m == 0:
-                count = stage.at[0, 0:7]
-            pltpu.make_async_copy(count, count, b_s).wait()
-        for m in range(8):
+        sent = stage.at[0, 0, 0:7]
+        pltpu.make_async_copy(sent, sent, b_s).wait()
+        sent = stage.at[0, 1]
+        pltpu.make_async_copy(sent, sent, b_s).wait()
+        for m in range(1, 8):
             pltpu.make_async_copy(stage.at[m], stage.at[m], b_s).wait()
 
 
@@ -538,9 +551,9 @@
             vm(24, 24, 256), vm(20, 24, 256), vm(20, 24, 256), vm(16, 24, 256), vm(16, 24, 256), vm(26, 32, 256),
             vm(400, 128), vm(8, 16, 128), vm(3, 64, 128), vm(192, 128),
             vm(8, 16, 40, 128), vm(8, 56, 128), vm(8, 56, 128), vm(8, 56, 128), vm(5, 8, 8, 128),
-            vm(8, 8, 3, 8, 128), vm(3, 128, 128), vm(128, 128),
-            dma(3), pltpu.SemaphoreType.DMA, pltpu.SemaphoreType.DMA,
-            dma(8), dma(8), dma(8), dma(8), dma(8), dma(8), dma(8), dma(8),
+            vm(8, 2, 8, 2, 8, 128), vm(2, 128, 128), vm(2, 128, 128),
+            dma(3), dma(2), dma(2),
+            dma(8), dma(8), dma(8), dma(8), dma(14), dma(14), dma(8), dma(8),
             pltpu.SemaphoreType.DMA, dma(8), dma(5), dma(5),
             pltpu.SemaphoreType.DMA, pltpu.SemaphoreType.DMA,
         ],

time: 68.6 us -> 67 us (0.977)
  Pallas kernels: 66.4 us -> 64.9 us
    pallas_call x1, Pallas kernels: 66.4 us -> 64.9 us  [local(): pl.pallas_call(kernel, out_shape=jax.ShapeDtypeStruct(guess.shape, F32),...]
where the time goes in v5:
time: 67 us; the launch traced here: 66.9 us
  Pallas kernels  64.9 us (97%)
  local copies, waits for them, and re-layouts  2.01 us (3%)
    pallas_call x1, Pallas kernels, local(): pl.pallas_call(kernel, out_shape=jax.ShapeDtypeStruct(guess.shape, F32),...  64.9 us
    unnamed x3, local copies, waits for them, and re-layouts  2.01 us

profile of v5, /device:TPU:27, one launch (start us, length us, event | category | flops | bytes accessed | tf_op | source)
XLA Modules:
  0.0 66.9 jit_solution(11140087131760259625)
XLA Ops:
  0.0 0.0 copy-start
  0.0 1.1 %copy-done = f32[3,1,16,16,256]{4,3,2,1,0:T(8,128)S(1)} copy-done((f32[3,1,16,16,256]{4,3,2,1,0:T(8,128)S(1)}, f32[3,1,16,16,256]{4,3,2,1,0:T(8,128)}, u32[]{:S(2)}) %copy-start) | copy-done | bytes 786456
  1.1 64.9 %shard_map.17 = f32[3,1,16,16,256]{4,3,2,1,0:T(8,128)S(1)} custom-call(f32[3,1,16,16,256]{4,3,2,1,0:T(8,128)S(1)} %copy-done), custom_call_target="tpu_custom_call" | custom-call | tf_op jit(solution)/shard_map/pallas_call | solution.py:537
  66.0 0.9 %copy.3 = f32[3,1,16,16,256]{4,3,2,1,0:T(8,128)} copy(f32[3,1,16,16,256]{4,3,2,1,0:T(8,128)S(1)} %shard_map.17) | data formatting | bytes 1572864
Async XLA Ops:
  0.0 1.1 %copy-start = (f32[3,1,16,16,256]{4,3,2,1,0:T(8,128)S(1)}, f32[3,1,16,16,256]{4,3,2,1,0:T(8,128)}, u32[]{:S(2)}) copy-start(f32[3,1,16,16,256]{4,3,2,1,0:T(8,128)} %g.1) | copy-start | bytes 2359300

commit v6 on v5

--- a/solution.py
+++ b/solution.py
@@ -210,10 +210,12 @@
     loop(16, mix_force, 4)
 
     def wide_halo(p, r, xs, xr, ys, yr, cs, cr, ss, rs):
-        ys[0, :, 0:4, :] = p[4:20, 16:20, :]
-        ys[0, :, 4:6, :] = r[2:18, 18:20, :]
-        ys[1, :, 0:4, :] = p[4:20, 4:8, :]
-        ys[1, :, 4:6, :] = r[2:18, 4:6, :]
+        for i in range(4):
+            layers, near, row = pl.ds(4 + 4 * i, 4), pl.ds(2 + 4 * i, 4), 6 * i
+            ys[0, :, row : row + 4, :] = p[layers, 16:20, :]
+            ys[0, :, row + 4 : row + 6, :] = r[near, 18:20, :]
+            ys[1, :, row : row + 4, :] = p[layers, 4:8, :]
+            ys[1, :, row + 4 : row + 6, :] = r[near, 4:6, :]
         xs[0, 0:4] = p[16:20, 4:20, :]
         xs[0, 4:6] = r[16:18, 4:20, :]
         xs[1, 0:4] = p[4:8, 4:20, :]
@@ -244,8 +246,9 @@
         p[20:24, 4:20, :] = xr[1, 0:4]
         r[18:20, 4:20, :] = xr[1, 4:6]
         for s, low, near in ((0, 0, 2), (1, 20, 20)):
-            p[4:20, low : low + 4, :] = yr[s, :, 0:4, :]
-            r[2:18, near : near + 2, :] = yr[s, :, 4:6, :]
+            for i in range(4):
+                p[4 + 4 * i : 8 + 4 * i, low : low + 4, :] = yr[s, :, 6 * i : 6 * i + 4, :]
+                r[2 + 4 * i : 6 + 4 * i, near : near + 2, :] = yr[s, :, 6 * i + 4 : 6 * i + 6, :]
         for k, (dx, dy) in enumerate(DIRS[4:]):
             for row, d, count in ((0, 1, 3), (3, 2, 2), (5, 3, 1)):
                 x = 4 - d if dx > 0 else 19 + d
@@ -330,12 +333,8 @@
     average([u21[x] for x in range(24)], 24)
     cb[1] = bricks(24, 4, 2)
     g1 = coarse_force(24, 0)
-    average([u22[x + 2] for x in range(16)], 24)
-    cb[2] = bricks(24, 4, 0)
-    average([j0[x] for x in range(16)], 24)
-    part0 = bricks(24, 4, 0)
-    average([j1[x] for x in range(16)], 24)
-    part1 = bricks(24, 4, 0)
+    average([j[x] for j in (j0, j1) for x in range(16)], 24)
+    part0, part1 = bricks(24, 4, 0), bricks(24, 4, 8)
     part0 = part0 + jnp.where(n == 0, cb[0], -HALF * g0)
     part1 = part1 - HALF * g1
     turned = jnp.transpose(jnp.concatenate([part0, part1], axis=0))
@@ -371,6 +370,9 @@
             @pl.when(is_chain)
             def _():
                 pltpu.make_async_copy(*part(me), g_r.at[n]).start()
+
+    average([u22[x + 2] for x in range(16)], 24)
+    cb[2] = bricks(24, 4, 0)
 
     lane = lax.broadcasted_iota(jnp.int32, (8, 128), 1)
     inner = lane & 7
@@ -483,11 +485,12 @@
     half[0] = jnp.transpose(back[0])
     half[1] = jnp.transpose(back[1])
     own_half = pl.ds(pl.multiple_of(64 * lax.rem(a, 2), 64), 64)
+    changes = [half[0, 0:64] - cb[0], half[0, 64:128] - cb[1], half[1, own_half] - cb[2]]
+    changes[0] = jnp.where(n == 0, 0.0, changes[0])
+    tall = dot(ydup[...], jnp.concatenate(changes, axis=1))
+    fines = dot(jnp.concatenate([tall[:, 128 * j : 128 * j + 128] for j in range(3)], axis=0), zdup[...])
     for j in range(3):
-        change = (half[0, 0:64], half[0, 64:128], half[1, own_half])[j] - cb[j]
-        if j == 0:
-            change = jnp.where(n == 0, 0.0, change)
-        fine = dot(dot(ydup[...], change), zdup[...])
+        fine = fines[128 * j : 128 * j + 128]
         for i in range(8):
             add = fine[16 * i : 16 * i + 16]
             for x in (2 * i, 2 * i + 1):
@@ -544,9 +547,9 @@
             vm(3, 20, 32, 256), vm(2, 16, 8, 256), vm(2, 16, 8, 256), vm(4, 1, 8, 256),
             vm(2, 20, 24, 256), vm(2, 20, 24, 256), vm(22, 24, 256), vm(22, 24, 256),
             vm(28, 32, 256), vm(4, 16, 256), vm(4, 16, 256), vm(24, 24, 256), vm(20, 24, 256),
-            vm(2, 6, 16, 256), vm(2, 6, 16, 256), vm(2, 16, 8, 256), vm(2, 16, 8, 256), vm(4, 8, 256), vm(4, 8, 256),
+            vm(2, 6, 16, 256), vm(2, 6, 16, 256), vm(2, 4, 24, 256), vm(2, 4, 24, 256), vm(4, 8, 256), vm(4, 8, 256),
             vm(24, 24, 256), vm(20, 24, 256), vm(24, 24, 256), vm(20, 24, 256),
-            vm(2, 6, 16, 256), vm(2, 6, 16, 256), vm(2, 16, 8, 256), vm(2, 16, 8, 256), vm(4, 8, 256), vm(4, 8, 256),
+            vm(2, 6, 16, 256), vm(2, 6, 16, 256), vm(2, 4, 24, 256), vm(2, 4, 24, 256), vm(4, 8, 256), vm(4, 8, 256),
             vm(20, 24, 256),
             vm(24, 24, 256), vm(20, 24, 256), vm(20, 24, 256), vm(16, 24, 256), vm(16, 24, 256), vm(26, 32, 256),
             vm(400, 128), vm(8, 16, 128), vm(3, 64, 128), vm(192, 128),

time: 67 us -> 67 us (level)
  no operation moved by 1% of the time
where the time goes in v6:
time: 67 us; the launch traced here: 66.9 us
  Pallas kernels  64.9 us (97%)
  local copies, waits for them, and re-layouts  2.01 us (3%)
    pallas_call x1, Pallas kernels, local(): pl.pallas_call(kernel, out_shape=jax.ShapeDtypeStruct(guess.shape, F32),...  64.9 us
    unnamed x3, local copies, waits for them, and re-layouts  2.01 us

profile of v6, /device:TPU:27, one launch (start us, length us, event | category | flops | bytes accessed | tf_op | source)
XLA Modules:
  0.0 66.9 jit_solution(10020459296498410271)
XLA Ops:
  0.0 0.0 copy-start
  0.0 1.1 %copy-done = f32[3,1,16,16,256]{4,3,2,1,0:T(8,128)S(1)} copy-done((f32[3,1,16,16,256]{4,3,2,1,0:T(8,128)S(1)}, f32[3,1,16,16,256]{4,3,2,1,0:T(8,128)}, u32[]{:S(2)}) %copy-start) | copy-done | bytes 786456
  1.1 64.9 %shard_map.17 = f32[3,1,16,16,256]{4,3,2,1,0:T(8,128)S(1)} custom-call(f32[3,1,16,16,256]{4,3,2,1,0:T(8,128)S(1)} %copy-done), custom_call_target="tpu_custom_call" | custom-call | tf_op jit(solution)/shard_map/pallas_call | solution.py:540
  66.0 0.9 %copy.3 = f32[3,1,16,16,256]{4,3,2,1,0:T(8,128)} copy(f32[3,1,16,16,256]{4,3,2,1,0:T(8,128)S(1)} %shard_map.17) | data formatting | bytes 1572864
Async XLA Ops:
  0.0 1.1 %copy-start = (f32[3,1,16,16,256]{4,3,2,1,0:T(8,128)S(1)}, f32[3,1,16,16,256]{4,3,2,1,0:T(8,128)}, u32[]{:S(2)}) copy-start(f32[3,1,16,16,256]{4,3,2,1,0:T(8,128)} %g.1) | copy-start | bytes 2359300

commit v7 on v6

--- a/solution.py
+++ b/solution.py
@@ -393,18 +393,25 @@
     def _():
         v0[...] = jnp.zeros_like(v0)
 
+        def two_bricks(m, t, r):
+            x, y = t // 4, t % 4
+            rows = pl.ds(r - 8, 8)
+            return gath[m, 8 * x + y, rows, :], gath[m, 8 * x + 4 + y, rows, :]
+
+        def first_part(m, t, r):
+            e, o = two_bricks(m, t, r)
+            return jnp.where(lane < 64, e, pltpu.roll(o, 64, 1))
+
+        def second_part(m, t, r):
+            e, o = two_bricks(m, t, r)
+            return jnp.where(lane < 64, pltpu.roll(e, 64, 1), o)
+
         def sweep(src, dst, m, first, inside, outside):
             def one(t, r, u, l):
                 m0[t, r : r + 8, :] = u * (u * u - 1.0) - l
 
             def two(t, r, u, f):
-                x, y = t // 4, t % 4
-                rows = pl.ds(r - 8, 8)
-                e, o = gath[m, 8 * x + y, rows, :], gath[m, 8 * x + 4 + y, rows, :]
-                if first:
-                    part = jnp.where(lane < 64, e, pltpu.roll(o, 64, 1))
-                else:
-                    part = jnp.where(lane < 64, pltpu.roll(e, 64, 1), o)
+                part = first_part(m, t, r) if first else second_part(m, t, r)
                 dst[t, r : r + 8, :] = src[t, r : r + 8, :] + HALF * f + part
 
             chain_lap(src, *inside, one)
@@ -462,7 +469,20 @@
                 whole = gath.at[m, :, pl.ds(low, length), :]
                 pltpu.make_async_copy(whole, whole, g_r.at[m]).wait()
                 begin = [v0[t, 24:32, :] for t in range(8)]
-                sweep(v0, v1, m, True, *spans[i][:2])
+                if i > 0:
+                    sweep(v0, v1, m, True, *spans[i][:2])
+                else:
+
+                    @pl.when(h == 0)
+                    def _():
+                        for t in range(8):
+                            for r in range(*full, 8):
+                                v1[t, r : r + 8, :] = first_part(m, t, r)
+
+                    @pl.when(h == 1)
+                    def _():
+                        sweep(v0, v1, m, True, *spans[0][:2])
+
                 for t in range(8):
                     middle = v1[t, 24:32, :]
                     stage[m, 0, t, 0] = jnp.where(lane < 64, begin[t], pltpu.roll(middle, 64, 1))

time: 67 us -> 66.8 us (level)
  no operation moved by 1% of the time
where the time goes in v7:
time: 66.8 us; the launch traced here: 66.7 us
  Pallas kernels  64.7 us (97%)
  local copies, waits for them, and re-layouts  2.01 us (3%)
    pallas_call x1, Pallas kernels, local(): pl.pallas_call(kernel, out_shape=jax.ShapeDtypeStruct(guess.shape, F32),...  64.7 us
    unnamed x3, local copies, waits for them, and re-layouts  2.01 us

profile of v7, /device:TPU:27, one launch (start us, length us, event | category | flops | bytes accessed | tf_op | source)
XLA Modules:
  0.0 66.7 jit_solution(14891196113228818999)
XLA Ops:
  0.0 0.0 copy-start
  0.0 1.1 %copy-done = f32[3,1,16,16,256]{4,3,2,1,0:T(8,128)S(1)} copy-done((f32[3,1,16,16,256]{4,3,2,1,0:T(8,128)S(1)}, f32[3,1,16,16,256]{4,3,2,1,0:T(8,128)}, u32[]{:S(2)}) %copy-start) | copy-done | bytes 786456
  1.1 64.7 %shard_map.17 = f32[3,1,16,16,256]{4,3,2,1,0:T(8,128)S(1)} custom-call(f32[3,1,16,16,256]{4,3,2,1,0:T(8,128)S(1)} %copy-done), custom_call_target="tpu_custom_call" | custom-call | tf_op jit(solution)/shard_map/pallas_call | solution.py:560
  65.8 0.9 %copy.3 = f32[3,1,16,16,256]{4,3,2,1,0:T(8,128)} copy(f32[3,1,16,16,256]{4,3,2,1,0:T(8,128)S(1)} %shard_map.17) | data formatting | bytes 1572864
Async XLA Ops:
  0.0 1.1 %copy-start = (f32[3,1,16,16,256]{4,3,2,1,0:T(8,128)S(1)}, f32[3,1,16,16,256]{4,3,2,1,0:T(8,128)}, u32[]{:S(2)}) copy-start(f32[3,1,16,16,256]{4,3,2,1,0:T(8,128)} %g.1) | copy-start | bytes 2359300
